TPU v7x, 128 devices: a whole 4x4x4 slice. The times are simulated.
128 devices in a mesh: gy: 16 (over y, x), gz: 8 (over z, core).
Axes of the slice: x: 4, y: 4, z: 4, core: 2. Of those that a mesh axis runs over, the one named last changes fastest.
Arguments:
- phase: bfloat16 [16, 512, 1024], P(None, 'gy', 'gz'), may hold values from 0 to 1
- undercool: bfloat16 [16, 512, 1024], P(None, 'gy', 'gz'), may hold values from -4 to 4
- perm_base: bfloat16 [16, 512, 1024], P(None, 'gy', 'gz'), may hold values from 0.5 to 10
- source: float32 [16, 512, 1024], P(None, 'gy', 'gz'), may hold values from -6 to 6
- pressure: float32 [16, 512, 1024], P(None, 'gy', 'gz'), may hold values from -6 to 6
Outputs:
- phase_next: bfloat16 [16, 512, 1024], P(None, 'gy', 'gz')
- pressure_next: float32 [16, 512, 1024], P(None, 'gy', 'gz')
- residual: float32 [16, 512, 1024], P(None, 'gy', 'gz')
All inputs are finite; a program needn't handle non-finite values.
Results may differ from a plain program's by a relative error of at most 0.0004.
Values may be sent and summed in bfloat16 or wider, within the bound.
A program may use at most 128 MiB of HBM per device.

v0:
```python
import jax
import jax.numpy as jnp
from jax import lax
from jax.sharding import PartitionSpec as P

LEVELS = 5
PRE = 2
POST = 2
COARSE_SWEEPS = 20


def extended(shard, sides, width):
    for axis, dim in sides:
        count, length = (lax.axis_size(axis), shard.shape[dim])
        up = [(i, (i + 1) % count) for i in range(count - 1)]
        down = [(j, i) for i, j in up]
        last = lax.slice_in_dim(shard, length - width, length, axis=dim)
        initial = lax.slice_in_dim(shard, 0, width, axis=dim)
        before = lax.ppermute(last, axis, up)
        after = lax.ppermute(initial, axis, down)
        shard = jnp.concatenate([before, shard, after], axis=dim)
    return shard


def pad_first(array):
    return jnp.pad(array, ((1, 1), (0, 0), (0, 0)))


def fine_pad(array):
    return pad_first(extended(array, (("gy", 1), ("gz", 2)), 1))


def second_pad(array):
    return pad_first(extended(array, (("gy", 1), ("gz", 2)), 1))


def third_pad(array):
    return pad_first(extended(array, (("gy", 1), ("gz", 2)), 1))


def fourth_pad(array):
    return pad_first(extended(array, (("gy", 1), ("gz", 2)), 1))


def coarse_pad(array):
    return pad_first(extended(array, (("gy", 1), ("gz", 2)), 1))


def shifted(padded):
    return (
        padded[2:, 1:-1, 1:-1],
        padded[:-2, 1:-1, 1:-1],
        padded[1:-1, 2:, 1:-1],
        padded[1:-1, :-2, 1:-1],
        padded[1:-1, 1:-1, 2:],
        padded[1:-1, 1:-1, :-2],
    )


def restrict(array):
    n_one, n_two, n_three = array.shape
    blocks = array.reshape(n_one // 2, 2, n_two // 2, 2, n_three // 2, 2)
    return jnp.sum(blocks, axis=(1, 3, 5)) * 0.125


def prolong(array):
    return jnp.repeat(jnp.repeat(jnp.repeat(array, 2, 0), 2, 1), 2, 2)


def parity(extent, offset_y, offset_z):
    parity_sum = (
        lax.broadcasted_iota(jnp.int32, extent, 0)
        + lax.broadcasted_iota(jnp.int32, extent, 1)
        + lax.broadcasted_iota(jnp.int32, extent, 2)
    )
    return (parity_sum + offset_y + offset_z) % 2 == 0


def face_sums(padded_iterate, conduct, padded_conduct):
    flux_sum = jnp.zeros(conduct.shape, jnp.float32)
    diag_sum = jnp.zeros(conduct.shape, jnp.float32)
    for near_value, near_coef in zip(shifted(padded_iterate), shifted(padded_conduct)):
        face_coef = 0.5 * (conduct + near_coef)
        flux_sum = flux_sum + face_coef * near_value
        diag_sum = diag_sum + face_coef
    return (flux_sum, diag_sum)


def half_sweep(iterate, right, level_data, red_cells):
    conduct, padded_conduct, factor, even_cells, pad_fn = level_data
    flux_sum, diag_sum = face_sums(pad_fn(iterate), conduct, padded_conduct)
    update = (right + factor * flux_sum) / (factor * diag_sum)
    return jnp.where(red_cells, update, iterate)


def red_black(iterate, right, level_data):
    even_cells = level_data[3]
    iterate = half_sweep(iterate, right, level_data, even_cells)
    return half_sweep(iterate, right, level_data, jnp.logical_not(even_cells))


def defect_of(iterate, right, level_data):
    conduct, padded_conduct, factor, even_cells, pad_fn = level_data
    flux_sum, diag_sum = face_sums(pad_fn(iterate), conduct, padded_conduct)
    return right - factor * (diag_sum * iterate - flux_sum)


def coarse_sweeps(iterate, right, level_data):
    return lax.fori_loop(
        0, COARSE_SWEEPS, lambda number, guess: red_black(guess, right, level_data), iterate
    )


def per_device(phase, undercool, perm_base, source, pressure):
    ice_now = phase.astype(jnp.float32)
    padded_ice = pad_first(extended(phase, (("gy", 1), ("gz", 2)), 1)).astype(jnp.float32)
    laplace = jnp.zeros_like(ice_now)
    for near_value in shifted(padded_ice):
        laplace = laplace + near_value
    laplace = laplace - 6.0 * ice_now
    well_term = 2.0 * ice_now * (1.0 - ice_now) * (1.0 - 2.0 * ice_now)
    drive_term = (
        30.0 * ice_now * ice_now * (1.0 - ice_now) * (1.0 - ice_now) * undercool.astype(jnp.float32)
    )
    ice_new = jnp.clip(ice_now + 0.12 * laplace - 0.5 * well_term + 0.25 * drive_term, 0.0, 1.0)
    phase_next = ice_new.astype(jnp.bfloat16)
    conduct = perm_base.astype(jnp.float32) * jnp.exp(-1.5 * ice_new)
    gy_index = lax.axis_index("gy")
    gz_index = lax.axis_index("gz")
    pad_list = (fine_pad, second_pad, third_pad, fourth_pad)
    coefs = [conduct]
    for depth in range(1, LEVELS):
        coefs.append(restrict(coefs[-1]))
    spread_limit = LEVELS - 1
    levels = []
    for depth in range(spread_limit):
        coef_here = coefs[depth]
        levels.append(
            (
                coef_here,
                pad_list[depth](coef_here),
                0.25**depth,
                parity(
                    coef_here.shape, gy_index * coef_here.shape[1], gz_index * coef_here.shape[2]
                ),
                pad_list[depth],
            )
        )
    coarse_coef = coefs[LEVELS - 1]
    coarse_factor = 0.25 ** (LEVELS - 1)

    def coarse_solve(right):
        level_data = (
            coarse_coef,
            coarse_pad(coarse_coef),
            coarse_factor,
            parity(
                coarse_coef.shape, gy_index * coarse_coef.shape[1], gz_index * coarse_coef.shape[2]
            ),
            coarse_pad,
        )
        return coarse_sweeps(jnp.zeros_like(right), right, level_data)

    def cycle(depth, right, iterate):
        if depth == spread_limit:
            return coarse_solve(right)
        level_data = levels[depth]
        for sweep in range(PRE):
            iterate = red_black(iterate, right, level_data)
        defect = restrict(defect_of(iterate, right, level_data))
        correction = cycle(depth + 1, defect, jnp.zeros_like(defect))
        iterate = iterate + prolong(correction)
        for sweep in range(POST):
            iterate = red_black(iterate, right, level_data)
        return iterate

    pressure_next = cycle(0, source, pressure)
    residual = defect_of(pressure_next, source, levels[0])
    return (phase_next, pressure_next, residual)


def solution(mesh):
    placed = (
        P(None, "gy", "gz"),
        P(None, "gy", "gz"),
        P(None, "gy", "gz"),
        P(None, "gy", "gz"),
        P(None, "gy", "gz"),
    )
    return jax.shard_map(
        per_device,
        mesh=mesh,
        in_specs=placed,
        out_specs=(P(None, "gy", "gz"), P(None, "gy", "gz"), P(None, "gy", "gz")),
        check_vma=False,
    )
```

profile of v0, /device:TPU:1, one launch (start us, length us, event | category | flops | bytes accessed | tf_op | source)
XLA Modules:
  0.0 1772.6 jit_solution(2829713941408253170)
XLA Ops:
  57.7 9.6 collective-permute-done.9
  120.1 10.0 fusion.128
  155.8 18.1 %reshape.222 = f32[8,2,16,2,64,2]{5,4,3,2,1,0:T(8,128)} reshape(f32[16,32,128]{2,1,0:T(8,128)S(1)} %copy.527) | data formatting | bytes 524288 | tf_op jit(solution)/shard_map/reshape | solution.py:62
  184.0 7.8 fusion.116
  292.2 18.1 %reshape.221 = f32[8,2,16,2,64,2]{5,4,3,2,1,0:T(8,128)} reshape(f32[16,32,128]{2,1,0:T(8,128)S(1)} %copy.526) | data formatting | bytes 524288 | tf_op jit(solution)/shard_map/reshape | solution.py:62
  613.2 757.0 %while.18 = (s32[]{:T(128)}, f32[1,2,8]{2,1,0:T(2,128)}, bf16[1,2,8]{2,1,0:T(2,128)(2,1)}, f32[1,2,8]{2,1,0:T(2,128)}, f32[1,2,8]{2,1,0:T(2,128)}, /*index=5*/f3...) while((s32[]{:T(128)}, f32[1,2,8]{2,1,0:T(2,128)}, ...), condition=%wide.wide.region_11.12_spmd.clone, body=%wide.wide.region_10.11_spmd.clone.sunk | while | flops 1907 | bytes 5756 | solution.py:109
  685.2 7.2 collective-permute-start.1
  723.4 7.2 collective-permute-start.1
  761.7 7.2 collective-permute-start.1
  799.9 7.2 collective-permute-start.1
  838.1 7.2 collective-permute-start.1
  876.3 7.2 collective-permute-start.1
  914.6 7.2 collective-permute-start.1
  952.8 7.2 collective-permute-start.1
  991.0 7.2 collective-permute-start.1
  1029.3 7.2 collective-permute-start.1
  1067.5 7.2 collective-permute-start.1
  1105.7 7.2 collective-permute-start.1
  1144.0 7.2 collective-permute-start.1
  1182.2 7.2 collective-permute-start.1
  1220.4 7.2 collective-permute-start.1
  1258.6 7.2 collective-permute-start.1
  1335.1 7.2 collective-permute-start.1
  1761.5 8.6 fusion.21
  (1550 shorter events, 1571.4 us)
Async XLA Ops:
  0.7 23.5 %collective-permute-start.89 = (f32[2,1,16]{2,1,0:T(1,128)S(1)}, f32[2,1,16]{2,1,0:T(1,128)S(1)}, u32[]{:S(2)}, u32[]{:S(2)}) collective-permute-start(f32[2,1,16]{2,1,0:T(1,128)S(1)} %broadcast.420), channel_id=1, source_target_pairs={{8,0},{16,8},{24,16},{32,24},{40,32},{48,40},{56,48},{64,56},{72,6... | collective-permute-start | bytes 392 | tf_op jit(solution)/shard_map/ppermute | solution.py:20
  2.1 26.1 %collective-permute-start.88 = (f32[2,1,16]{2,1,0:T(1,128)S(1)}, f32[2,1,16]{2,1,0:T(1,128)S(1)}, u32[]{:S(2)}, u32[]{:S(2)}) collective-permute-start(f32[2,1,16]{2,1,0:T(1,128)S(1)} %broadcast.420), channel_id=1, source_target_pairs={{0,8},{8,16},{16,24},{24,32},{32,40},{40,48},{48,56},{56,64},{64,7... | collective-permute-start | bytes 392 | tf_op jit(solution)/shard_map/ppermute | solution.py:19
  6.7 22.9 %collective-permute-start.65 = (f32[4,1,32]{2,1,0:T(1,128)S(1)}, f32[4,1,32]{2,1,0:T(1,128)S(1)}, u32[]{:S(2)}, u32[]{:S(2)}) collective-permute-start(f32[4,1,32]{2,1,0:T(1,128)S(1)} %broadcast.415), channel_id=1, source_target_pairs={{8,0},{16,8},{24,16},{32,24},{40,32},{48,40},{56,48},{64,56},{72,6... | collective-permute-start | bytes 1544 | tf_op jit(solution)/shard_map/ppermute | solution.py:20
  8.0 26.1 %collective-permute-start.64 = (f32[4,1,32]{2,1,0:T(1,128)S(1)}, f32[4,1,32]{2,1,0:T(1,128)S(1)}, u32[]{:S(2)}, u32[]{:S(2)}) collective-permute-start(f32[4,1,32]{2,1,0:T(1,128)S(1)} %broadcast.415), channel_id=1, source_target_pairs={{0,8},{8,16},{16,24},{24,32},{32,40},{40,48},{48,56},{56,64},{64,7... | collective-permute-start | bytes 1544 | tf_op jit(solution)/shard_map/ppermute | solution.py:19
  22.8 28.3 %collective-permute-start.41 = (f32[8,1,64]{2,1,0:T(1,128)S(1)}, f32[8,1,64]{2,1,0:T(1,128)S(1)}, u32[]{:S(2)}, u32[]{:S(2)}) collective-permute-start(f32[8,1,64]{2,1,0:T(1,128)S(1)} %broadcast.410), channel_id=1, source_target_pairs={{8,0},{16,8},{24,16},{32,24},{40,32},{48,40},{56,48},{64,56},{72,6... | collective-permute-start | bytes 6152 | tf_op jit(solution)/shard_map/ppermute | solution.py:20
  24.2 33.4 %collective-permute-start.40 = (f32[8,1,64]{2,1,0:T(1,128)S(1)}, f32[8,1,64]{2,1,0:T(1,128)S(1)}, u32[]{:S(2)}, u32[]{:S(2)}) collective-permute-start(f32[8,1,64]{2,1,0:T(1,128)S(1)} %broadcast.410), channel_id=1, source_target_pairs={{0,8},{8,16},{16,24},{24,32},{32,40},{40,48},{48,56},{56,64},{64,7... | collective-permute-start | bytes 6152 | tf_op jit(solution)/shard_map/ppermute | solution.py:19
  28.3 71.4 %collective-permute-start.17 = (f32[16,1,128]{2,0,1:T(8,128)S(1)}, f32[16,1,128]{2,0,1:T(8,128)S(1)}, u32[]{:S(2)}, u32[]{:S(2)}) collective-permute-start(f32[16,1,128]{2,0,1:T(8,128)S(1)} %bitcast.194), channel_id=1, source_target_pairs={{8,0},{16,8},{24,16},{32,24},{40,32},{48,40},{56,48},{64,56},{72,6... | collective-permute-start | bytes 24584 | tf_op jit(solution)/shard_map/ppermute | solution.py:20
  44.0 48.0 %collective-permute-start.16 = (f32[16,1,128]{2,0,1:T(8,128)}, f32[16,1,128]{2,0,1:T(8,128)S(1)}, u32[]{:S(2)}, u32[]{:S(2)}) collective-permute-start(f32[16,1,128]{2,0,1:T(8,128)} %bitcast.55), channel_id=1, source_target_pairs={{0,8},{8,16},{16,24},{24,32},{32,40},{40,48},{48,56},{56,64},{64,7... | collective-permute-start | bytes 24584 | tf_op jit(solution)/shard_map/ppermute | solution.py:19
  74.7 68.2 %collective-permute-start.43 = (f32[8,18,1]{2,0,1:T(8,128)S(1)}, f32[8,18,1]{2,0,1:T(8,128)S(1)}, u32[]{:S(2)}, u32[]{:S(2)}) collective-permute-start(f32[8,18,1]{2,0,1:T(8,128)S(1)} %get-tuple-element.389), channel_id=1, source_target_pairs={{1,0},{2,1},{3,2},{4,3},{5,4},{6,5},{7,6},{9,8},{10,9},{11,10},{12... | collective-permute-start | bytes 1736 | tf_op jit(solution)/shard_map/ppermute | solution.py:20
  76.7 66.1 %collective-permute-start.42 = (f32[8,18,1]{2,0,1:T(8,128)S(1)}, f32[8,18,1]{2,0,1:T(8,128)S(1)}, u32[]{:S(2)}, u32[]{:S(2)}) collective-permute-start(f32[8,18,1]{2,0,1:T(8,128)S(1)} %get-tuple-element.390), channel_id=1, source_target_pairs={{0,1},{1,2},{2,3},{3,4},{4,5},{5,6},{6,7},{8,9},{9,10},{10,11},{11... | collective-permute-start | bytes 1736 | tf_op jit(solution)/shard_map/ppermute | solution.py:19
  90.7 19.0 %collective-permute-start.13 = (f32[16,1,128]{2,0,1:T(8,128)S(1)}, f32[16,1,128]{2,0,1:T(8,128)S(1)}, u32[]{:S(2)}, u32[]{:S(2)}) collective-permute-start(f32[16,1,128]{2,0,1:T(8,128)S(1)} %copy.482), channel_id=1, source_target_pairs={{8,0},{16,8},{24,16},{32,24},{40,32},{48,40},{56,48},{64,56},{72,6... | collective-permute-start | bytes 24584 | tf_op jit(solution)/shard_map/ppermute | solution.py:20
  147.4 33.5 %collective-permute-start.23 = (f32[16,34,1]{1,0,2:T(8,128)S(1)}, f32[16,34,1]{1,0,2:T(8,128)S(1)}, u32[]{:S(2)}, u32[]{:S(2)}) collective-permute-start(f32[16,34,1]{1,0,2:T(8,128)S(1)} %get-tuple-element.319), channel_id=1, source_target_pairs={{1,0},{2,1},{3,2},{4,3},{5,4},{6,5},{7,6},{9,8},{10,9},{11,10},{12... | collective-permute-start | bytes 6536 | tf_op jit(solution)/shard_map/ppermute | solution.py:20
  149.3 31.6 %collective-permute-start.22 = (f32[16,34,1]{1,0,2:T(8,128)S(1)}, f32[16,34,1]{1,0,2:T(8,128)S(1)}, u32[]{:S(2)}, u32[]{:S(2)}) collective-permute-start(f32[16,34,1]{1,0,2:T(8,128)S(1)} %get-tuple-element.320), channel_id=1, source_target_pairs={{0,1},{1,2},{2,3},{3,4},{4,5},{5,6},{6,7},{8,9},{9,10},{10,11},{11... | collective-permute-start | bytes 6536 | tf_op jit(solution)/shard_map/ppermute | solution.py:19
  215.1 25.3 %collective-permute-start.36 = (f32[8,1,64]{2,1,0:T(1,128)S(1)}, f32[8,1,64]{2,1,0:T(1,128)S(1)}, u32[]{:S(2)}, u32[]{:S(2)}) collective-permute-start(f32[8,1,64]{2,1,0:T(1,128)S(1)} %get-tuple-element.407), channel_id=1, source_target_pairs={{0,8},{8,16},{16,24},{24,32},{32,40},{40,48},{48,56},{56,64},{64,7... | collective-permute-start | bytes 6152 | tf_op jit(solution)/shard_map/ppermute | solution.py:19
  221.3 19.1 %collective-permute-start.37 = (f32[8,1,64]{2,1,0:T(1,128)S(1)}, f32[8,1,64]{2,1,0:T(1,128)S(1)}, u32[]{:S(2)}, u32[]{:S(2)}) collective-permute-start(f32[8,1,64]{2,1,0:T(1,128)S(1)} %get-tuple-element.408), channel_id=1, source_target_pairs={{8,0},{16,8},{24,16},{32,24},{40,32},{48,40},{56,48},{64,56},{72,6... | collective-permute-start | bytes 6152 | tf_op jit(solution)/shard_map/ppermute | solution.py:20
  251.4 21.7 %collective-permute-start.38 = (f32[8,18,1]{2,0,1:T(8,128)}, f32[8,18,1]{2,0,1:T(8,128)S(1)}, u32[]{:S(2)}, u32[]{:S(2)}) collective-permute-start(f32[8,18,1]{2,0,1:T(8,128)} %get-tuple-element.385), channel_id=1, source_target_pairs={{0,1},{1,2},{2,3},{3,4},{4,5},{5,6},{6,7},{8,9},{9,10},{10,11},{11... | collective-permute-start | bytes 1736 | tf_op jit(solution)/shard_map/ppermute | solution.py:19
  253.3 19.7 %collective-permute-start.39 = (f32[8,18,1]{2,0,1:T(8,128)S(1)}, f32[8,18,1]{2,0,1:T(8,128)S(1)}, u32[]{:S(2)}, u32[]{:S(2)}) collective-permute-start(f32[8,18,1]{2,0,1:T(8,128)S(1)} %get-tuple-element.386), channel_id=1, source_target_pairs={{1,0},{2,1},{3,2},{4,3},{5,4},{6,5},{7,6},{9,8},{10,9},{11,10},{12... | collective-permute-start | bytes 1736 | tf_op jit(solution)/shard_map/ppermute | solution.py:20
  347.5 20.2 %collective-permute-start.48 = (f32[8,1,64]{2,1,0:T(1,128)}, f32[8,1,64]{2,1,0:T(1,128)}, u32[]{:S(2)}, u32[]{:S(2)}) collective-permute-start(f32[8,1,64]{2,1,0:T(1,128)} %get-tuple-element.403), channel_id=1, source_target_pairs={{0,8},{8,16},{16,24},{24,32},{32,40},{40,48},{48,56},{56,64},{64,7... | collective-permute-start | bytes 6152 | tf_op jit(solution)/shard_map/ppermute | solution.py:19
  357.1 29.0 %collective-permute-start.60 = (f32[4,1,32]{2,1,0:T(1,128)}, f32[4,1,32]{2,1,0:T(1,128)}, u32[]{:S(2)}, u32[]{:S(2)}) collective-permute-start(f32[4,1,32]{2,1,0:T(1,128)} %get-tuple-element.465), channel_id=1, source_target_pairs={{0,8},{8,16},{16,24},{24,32},{32,40},{40,48},{48,56},{56,64},{64,7... | collective-permute-start | bytes 1544 | tf_op jit(solution)/shard_map/ppermute | solution.py:19
  363.9 22.2 %collective-permute-start.61 = (f32[4,1,32]{2,1,0:T(1,128)}, f32[4,1,32]{2,1,0:T(1,128)}, u32[]{:S(2)}, u32[]{:S(2)}) collective-permute-start(f32[4,1,32]{2,1,0:T(1,128)} %get-tuple-element.466), channel_id=1, source_target_pairs={{8,0},{16,8},{24,16},{32,24},{40,32},{48,40},{56,48},{64,56},{72,6... | collective-permute-start | bytes 1544 | tf_op jit(solution)/shard_map/ppermute | solution.py:20
  445.3 55.1 %collective-permute-start.84 = (f32[2,1,16]{2,1,0:T(1,128)}, f32[2,1,16]{2,1,0:T(1,128)}, u32[]{:S(2)}, u32[]{:S(2)}) collective-permute-start(f32[2,1,16]{2,1,0:T(1,128)} %get-tuple-element.505), channel_id=1, source_target_pairs={{0,8},{8,16},{16,24},{24,32},{32,40},{40,48},{48,56},{56,64},{64,7... | collective-permute-start | bytes 392 | tf_op jit(solution)/shard_map/ppermute | solution.py:19
  449.8 50.5 %collective-permute-start.85 = (f32[2,1,16]{2,1,0:T(1,128)}, f32[2,1,16]{2,1,0:T(1,128)}, u32[]{:S(2)}, u32[]{:S(2)}) collective-permute-start(f32[2,1,16]{2,1,0:T(1,128)} %get-tuple-element.506), channel_id=1, source_target_pairs={{8,0},{16,8},{24,16},{32,24},{40,32},{48,40},{56,48},{64,56},{72,6... | collective-permute-start | bytes 392 | tf_op jit(solution)/shard_map/ppermute | solution.py:20
  491.4 86.1 %collective-permute-start.107 = (f32[1,4,1]{2,1,0:T(4,128)}, f32[1,4,1]{2,1,0:T(4,128)}, u32[]{:S(2)}, u32[]{:S(2)}) collective-permute-start(f32[1,4,1]{2,1,0:T(4,128)} %get-tuple-element.509), channel_id=1, source_target_pairs={{0,1},{1,2},{2,3},{3,4},{4,5},{5,6},{6,7},{8,9},{9,10},{10,11},{11... | collective-permute-start | bytes 56 | tf_op jit(solution)/shard_map/ppermute | solution.py:19
  538.3 39.2 %collective-permute-start.106 = (f32[1,4,1]{2,1,0:T(4,128)}, f32[1,4,1]{2,1,0:T(4,128)S(1)}, u32[]{:S(2)}, u32[]{:S(2)}) collective-permute-start(f32[1,4,1]{2,1,0:T(4,128)} %get-tuple-element.510), channel_id=1, source_target_pairs={{1,0},{2,1},{3,2},{4,3},{5,4},{6,5},{7,6},{9,8},{10,9},{11,10},{12... | collective-permute-start | bytes 56 | tf_op jit(solution)/shard_map/ppermute | solution.py:20
  (452 other events, 4384.1 us)
where the time goes:
time: 1800 us; the launch traced here: 1770 us
  starting transfers between devices  1120 us (62%)
  other arithmetic  257 us (14%)
  local copies, waits for them, and re-layouts  213 us (12%)
  waiting for transfers between devices  180 us (10%)
    ppermute x166, starting transfers between devices, extended(): before = lax.ppermute(last, axis, up)  843 us
    ppermute x166, starting transfers between devices, extended(): after = lax.ppermute(initial, axis, down)  272 us
    ppermute x166, waiting for transfers between devices, extended(): after = lax.ppermute(initial, axis, down)  133 us
    select_n x72, other arithmetic, half_sweep(): return jnp.where(red_cells, update, iterate)  99.5 us
    concatenate x224, other arithmetic, extended(): shard = jnp.concatenate([before, shard, after], axis=dim)  89.4 us
    slice x111, local copies, waits for them, and re-layouts, extended(): last = lax.slice_in_dim(shard, length - width, length, axis=dim)  55.5 us
    ppermute x166, waiting for transfers between devices, extended(): before = lax.ppermute(last, axis, up)  46.4 us
    reshape x4, local copies, waits for them, and re-layouts, restrict(): blocks = array.reshape(n_one // 2, 2, n_two // 2, 2, n_three // 2, 2)  42.1 us
  transfers between devices with their start and end apart: 332, of which 117 were waited for; matrix products, arithmetic and copies ran while one was open for 10% of the time, Pallas kernels for 0%

commit v1 on v0

v1 whole, which is shorter than its diff:
```python
import functools
import jax
import jax.numpy as jnp
from jax import lax
from jax.experimental import pallas as pl
from jax.experimental.pallas import tpu as pltpu
from jax.sharding import PartitionSpec as P

MESH = pl.DeviceIdType.MESH
F32 = jnp.float32
BF16 = jnp.bfloat16
COARSE_SWEEPS = 20
NX, NY, NZ = 16, 32, 128
HY = 8
R0 = NY + 2 * HY
R1 = 24
R2 = 14
NEAR = [(dy, dz) for dy in (-1, 0, 1) for dz in (-1, 0, 1) if (dy, dz) != (0, 0)]
X_IN, X_F, X_K, X_B1, X_V0, X_B2 = range(6)
N_X = 6


def roll(x, shift, axis):
    size = x.shape[axis]
    shift = shift % size
    return x if shift == 0 else pltpu.roll(x, shift, axis)


def loop(lo, hi, body, step=2):
    def trip(i, carry):
        for j in range(step):
            body(lo + i * step + j, j)
        return carry

    lax.fori_loop(0, (hi - lo) // step, trip, 0)


def kernel(
    GY, GZ, phase_h, under_h, perm_h, src_h, pres_h, phase_o, pres_o, res_o,
    inb, inf, tmp, pb, outb,
    ha, hf, zp, zpf, zb, zbf,
    ice, und, prm, S0, V0, K0, G0, BD0, D0, zv,
    KX, BX, CX, K1, V1, G1, I1, BD1, D1, K2, V2, G2, I2, BD2, D2,
    msg_k, msg_b, GK, GB, K3, G3, I3, D3, buf4, e3x, pair2,
    ssem, rsem, gs, gr, lsem, osem,
):
    gy, gz = lax.axis_index("gy"), lax.axis_index("gz")
    me = gy * GZ + gz

    def peer(dy, dz):
        return (lax.rem(gy + dy + GY, GY), lax.rem(gz + dz + GZ, GZ))

    barrier = pltpu.get_barrier_semaphore()

    def other(i):
        q = lax.rem(me + i, GY * GZ)
        return (q // GZ, lax.rem(q, GZ))

    def greet(i, carry):
        pl.semaphore_signal(barrier, inc=1, device_id=other(i), device_id_type=MESH)
        return carry

    lax.fori_loop(1, GY * GZ, greet, 0)

    loads = []
    for n, (src, dst) in enumerate(
        ((phase_h, inb.at[0]), (under_h, inb.at[1]), (perm_h, inb.at[2]), (src_h, inf.at[0]), (pres_h, inf.at[1]))
    ):
        copy = pltpu.make_async_copy(src, dst, lsem.at[n])
        copy.start()
        loads.append(copy)

    lane = lax.broadcasted_iota(jnp.int32, (8, 128), 1)
    sub = lax.broadcasted_iota(jnp.int32, (8, 128), 0)
    lane2 = lax.broadcasted_iota(jnp.int32, (8, 256), 1)
    sub2 = lax.broadcasted_iota(jnp.int32, (8, 256), 0)
    odd = lane % 2 == 1
    odd2 = lane2 % 2 == 1
    right_in, left_in = gz < GZ - 1, gz > 0
    up_in, down_in = gy > 0, gy < GY - 1
    ring_in = (lane2 < 128) | ((lane2 < 192) & right_in) | ((lane2 >= 192) & left_in)

    def cat(a, b):
        return jnp.concatenate([a, b], axis=-1)

    def ring(o, d):
        a, b = o[:, :128], o[:, 128:]
        fa, fb = roll(a, -d, 1), roll(b, -d, 1)
        ba, bb = roll(a, d, 1), roll(b, d, 1)
        end, start = lane >= 128 - d, lane < d
        ahead = cat(jnp.where(end, fb, fa), jnp.where(end, fa, fb))
        behind = cat(jnp.where(start, bb, ba), jnp.where(start, ba, bb))
        return ahead, behind

    for copy in loads:
        copy.wait()
    for n in range(3):
        for x in range(NX):
            tmp[n, pl.ds(x * NY, NY), :] = inb[n, x].astype(F32)
    for n in range(2):
        for x in range(NX):
            tmp[3 + n, pl.ds(x * NY, NY), :] = inf[n, x]

    def red_black_of(n, y, j):
        even = tmp[n, pl.ds(y, 8, stride=2 * NY), :]
        odds = tmp[n, pl.ds(NY + y, 8, stride=2 * NY), :]
        par = odd if j % 2 == 0 else jnp.logical_not(odd)
        return jnp.where(par, odds, even), jnp.where(par, even, odds)

    zp[...] = jnp.zeros_like(zp)
    zpf[...] = jnp.zeros_like(zpf)

    def prepare(k, carry):
        packed = jnp.zeros((48, 128), F32)
        packed_f = jnp.zeros((24, 128), F32)
        group = lax.broadcasted_iota(jnp.int32, (48, 128), 1) // 16
        for q in range(8):
            y = 8 * k + q
            parts = []
            for n in range(3):
                parts.extend(red_black_of(n, y, q))
            row = jnp.concatenate(parts, axis=0)
            ha[HY + y] = row.astype(BF16)
            s_r, s_b = red_black_of(3, y, q)
            _, v_b = red_black_of(4, y, q)
            row_f = jnp.concatenate([s_r, s_b, v_b], axis=0)
            hf[HY + y] = row_f
            packed = jnp.where(group == q, roll(row, 16 * q + 8, 1), packed)
            packed_f = jnp.where(group[:24] == q, roll(row_f, 16 * q + 8, 1), packed_f)
        zp[k] = packed.astype(BF16)
        zpf[k] = packed_f
        return carry

    lax.fori_loop(0, 4, prepare, 0)

    pl.semaphore_wait(barrier, GY * GZ - 1)

    def exchange(ex, pieces):
        copies = []
        for n, (dy, dz) in enumerate(NEAR):
            src, dst = pieces(dy, dz)
            copy = pltpu.make_async_remote_copy(
                src, dst, ssem.at[ex, n], rsem.at[ex, n], device_id=peer(dy, dz), device_id_type=MESH
            )
            copy.start()
            copies.append(copy)
        return copies

    def received(copies):
        for copy in copies:
            copy.wait_recv()

    def input_pieces(rows, packed, landing, width):
        def pieces(dy, dz):
            if dz == 0 and dy < 0:
                return rows.at[pl.ds(HY, width)], rows.at[pl.ds(HY + NY, width)]
            if dz == 0:
                return rows.at[pl.ds(HY + NY - width, width)], rows.at[pl.ds(HY - width, width)]
            side = 0 if dz > 0 else 1
            if dy == 0:
                return packed, landing.at[side, pl.ds(1, 4)]
            if dy > 0:
                return packed.at[pl.ds(3, 1)], landing.at[side, pl.ds(0, 1)]
            return packed.at[pl.ds(0, 1)], landing.at[side, pl.ds(5, 1)]

        return pieces

    x_in = exchange(X_IN, input_pieces(ha, zp, zb, 6))
    x_f = exchange(X_F, input_pieces(hf, zpf, zbf, 5))

    zero_row = jnp.zeros((8, 256), F32)
    e3x[...] = jnp.zeros_like(e3x)
    for c in range(2):
        for r in (0, R2 - 1):
            K2[c, r] = zero_row
            V2[c, r] = zero_row
        for r in (0, 1, R1 - 2, R1 - 1):
            V1[c, r] = zero_row
        for r in (3, R0 - 4):
            V0[c, r] = zero_row

    received(x_in)
    received(x_f)

    def row_mask(r, width):
        ok = ((r >= HY) | up_in) & ((r < HY + NY) | down_in)
        lanes = (lane2 < 128) | ((lane2 < 128 + width) & right_in) | ((lane2 >= 256 - width) & left_in)
        return lanes & ok

    def unpack(k, carry):
        group = lax.broadcasted_iota(jnp.int32, (48, 128), 1) % 16 < 8
        merged = jnp.where(group, zb[0, k].astype(F32), zb[1, k].astype(F32))
        merged_f = jnp.where(group[:24], zbf[0, k], zbf[1, k])
        for q in range(8):
            r = 8 * k + q
            ok = row_mask(r, 6) & (r >= 2) & (r < R0 - 2)
            ok5 = row_mask(r, 5) & (r >= 3) & (r < R0 - 3)
            side = roll(merged, 120 - 16 * q, 1)
            side_f = roll(merged_f, 120 - 16 * q, 1)
            a = ha[r].astype(F32)
            f = hf[r]
            for c in range(2):
                s = slice(8 * c, 8 * c + 8)
                ice[c, r] = jnp.where(ok, cat(a[s], side[s]), 0.0)
                s = slice(16 + 8 * c, 24 + 8 * c)
                und[c, r] = cat(a[s], side[s])
                s = slice(32 + 8 * c, 40 + 8 * c)
                prm[c, r] = jnp.where(ok5, cat(a[s], side[s]), 0.0)
                s = slice(8 * c, 8 * c + 8)
                S0[c, r] = cat(f[s], side_f[s])
            V0[1, r] = jnp.where(ok5, cat(f[16:24], side_f[16:24]), 0.0)
        return carry

    lax.fori_loop(0, 6, unpack, 0)

    def pick(c, j):
        return odd2 if (c + j) % 2 == 0 else jnp.logical_not(odd2)

    def x_outer(o, take):
        return jnp.where(take, roll(o, -1, 0), roll(o, 1, 0))

    def x_edge(take):
        return jnp.where(take, sub2, 7 - sub2) == 7

    def near0(ref, c, r, j):
        o = ref[1 - c, r]
        take = pick(c, j)
        ahead, behind = ring(o, 1)
        return (ref[1 - c, r - 1], ref[1 - c, r + 1], o, x_outer(o, take), ahead, behind)

    def permeability(r, j):
        for c in range(2):
            now = ice[c, r]
            near = list(near0(ice, c, r, j))
            near[3] = jnp.where(x_edge(pick(c, j)), 0.0, near[3])
            lap = near[0]
            for value in near[1:]:
                lap = lap + value
            lap = lap - 6.0 * now
            well = 2.0 * now * (1.0 - now) * (1.0 - 2.0 * now)
            drive = 30.0 * now * now * (1.0 - now) * (1.0 - now) * und[c, r]
            new = jnp.clip(now + 0.12 * lap - 0.5 * well + 0.25 * drive, 0.0, 1.0)
            K0[c, r] = jnp.where(prm[c, r] > 0.0, prm[c, r] * jnp.exp(-1.5 * new), 0.0)
            und[c, r] = new

    loop(2, R0 - 2, permeability)

    def swap_lanes(x, d):
        return jnp.where((lax.broadcasted_iota(jnp.int32, x.shape, 1) // d) % 2 == 0, roll(x, -d, 1), roll(x, d, 1))

    def swap_subs(x, d):
        return jnp.where((lax.broadcasted_iota(jnp.int32, x.shape, 0) // d) % 2 == 0, roll(x, -d, 0), roll(x, d, 0))

    def parity_y(level, ln, sb):
        return (sb // (1 if level == 1 else 2) + ln // (2 if level == 1 else 4)) % 2 == 1

    def own0(c, r):
        return K0[c, r, :, :128]

    def coarse0(y):
        r = HY + 2 * y
        t = (own0(0, r) + own0(1, r)) + (own0(0, r + 1) + own0(1, r + 1))
        return 0.125 * (t + swap_lanes(t, 1))

    p1, p2 = parity_y(1, lane, sub), parity_y(2, lane, sub)

    def split(p, low, high):
        return jnp.where(p, high, low), jnp.where(p, low, high)

    k2_rows = []
    for yp in range(8):
        red, black = split(p1, coarse0(2 * yp), coarse0(2 * yp + 1))
        KX[1, 1, yp] = jnp.where(odd, black, red)
        t = red + black
        t = t + swap_subs(t, 1)
        k2_rows.append(0.125 * (t + swap_lanes(t, 2)))
    k3_rows = []
    for yp in range(4):
        red, black = split(p2, k2_rows[2 * yp], k2_rows[2 * yp + 1])
        KX[1, 1, 8 + yp] = jnp.where(odd, black, red)
        t = red + black
        t = t + swap_subs(t, 2)
        k3_rows.append(0.125 * (t + swap_lanes(t, 4)))

    def block_pieces(ref):
        return lambda dy, dz: (ref.at[1, 1], ref.at[1 - dy, 1 - dz])

    x_k = exchange(X_K, block_pieces(KX))

    squeeze = (
        lax.broadcasted_iota(jnp.int32, (128, 128), 0) == 8 * (lax.broadcasted_iota(jnp.int32, (128, 128), 1) % 16)
    ).astype(F32)

    def dot(a, b):
        return lax.dot_general(
            a, b, (((1,), (0,)), ((), ())), precision=lax.Precision.HIGHEST, preferred_element_type=F32
        )

    def message(rows):
        piece = jnp.zeros((8, 128), F32)
        for y in range(4):
            u = rows[y]
            t = jnp.where((y + lane // 8) % 2 == 0, u, roll(u, 4, 0))
            piece = jnp.where(sub % 4 == y, t, piece)
        wide = dot(piece, squeeze)
        return jnp.sum(jnp.where(lane // 16 == sub, wide, 0.0), axis=0, keepdims=True)

    def gather(msg, landing, n, row):
        msg[0] = row
        landing[pl.ds(me, 1)] = row.reshape(1, 1, 128)

        def send(i, carry):
            pltpu.make_async_remote_copy(
                msg, landing.at[pl.ds(me, 1)], gs.at[n], gr.at[n], device_id=other(i), device_id_type=MESH
            ).start()
            return carry

        lax.fori_loop(1, GY * GZ, send, 0)

    def all_bytes(landing, sem):
        part = landing.at[pl.ds(0, GY * GZ - 1)]
        pltpu.make_async_copy(part, part, sem).wait()

    def global_level3(landing):
        x = landing[...].reshape(GY, GZ, 128)
        ln = lax.broadcasted_iota(jnp.int32, x.shape, 2)
        sb = lax.broadcasted_iota(jnp.int32, x.shape, 1)
        for bit in (1, 2, 4):
            s_set, t_set = (sb // bit) % 2 == 1, (ln // (16 * bit)) % 2 == 1
            down = roll(roll(x, bit, 1), -16 * bit, 2)
            up = roll(roll(x, -bit, 1), 16 * bit, 2)
            x = jnp.where(s_set == t_set, x, jnp.where(s_set, down, up))
        pairs = x.reshape(GY // 2, 2, 8, 128)
        even, odds = pairs[:, 0], pairs[:, 1]
        low = lax.broadcasted_iota(jnp.int32, even.shape, 1) < 4
        red = jnp.where(low, even, roll(odds, 4, 1))
        black = jnp.where(low, roll(even, 4, 1), odds)
        return red.reshape(64, 128), black.reshape(64, 128)

    gather(msg_k, GK, 0, message(k3_rows))

    def faces0(r, j):
        ok = row_mask(r, 5)
        for c in range(2):
            k = K0[c, r]
            take = pick(c, j)
            edge = x_edge(take)
            near = list(near0(K0, c, r, j))
            near[3] = jnp.where(edge, 0.0, near[3])
            f = [0.5 * (k + value) for value in near]
            d = ((f[0] + f[1]) + (f[2] + f[3])) + (f[4] + f[5])
            inv = jnp.where(ok, 1.0 / d, 0.0)
            for n in range(6):
                g = f[n] * inv
                G0[c, r, n] = jnp.where(edge, 0.0, g) if n == 3 else g
            BD0[c, r] = jnp.where(ok, S0[c, r], 0.0) * inv
            D0[c, r] = d

    loop(4, R0 - 4, faces0)

    def update0(c, r, j):
        near = near0(V0, c, r, j)
        t = [G0[c, r, n] * near[n] for n in range(6)]
        return BD0[c, r] + (((t[0] + t[1]) + (t[2] + t[3])) + (t[4] + t[5]))

    def sweep0(c, lo, hi):
        def body(r, j):
            V0[c, r] = update0(c, r, j)

        loop(lo, hi, body)

    sweep0(0, 4, R0 - 4)
    sweep0(1, 4, R0 - 4)
    sweep0(0, 6, R0 - 6)
    sweep0(1, 6, R0 - 6)

    def defect0(r, j):
        return (D0[0, r] * (update0(0, r, j) - V0[0, r]))[:, :128]

    def right1(yp, carry):
        rows = []
        for j in range(2):
            r = HY + 4 * yp + 2 * j
            t = defect0(r, 0) + defect0(r + 1, 1)
            rows.append(0.125 * (t + swap_lanes(t, 1)))
        red, black = split(p1, rows[0], rows[1])
        BX[1, 1, yp] = jnp.where(odd, black, red)
        return carry

    lax.fori_loop(0, 8, right1, 0)
    x_b1 = exchange(X_B1, block_pieces(BX))

    received(x_k)

    def joined(ref, yb, r):
        a = ref[yb, 1, r]
        b = jnp.where(lane < 64, ref[yb, 2, r], ref[yb, 0, r])
        return cat(a, b)

    def apart(x):
        a, b = x[:, :128], x[:, 128:]
        red = cat(jnp.where(odd, roll(a, 1, 1), a), jnp.where(odd, roll(b, 1, 1), b))
        black = cat(jnp.where(odd, a, roll(a, -1, 1)), jnp.where(odd, b, roll(b, -1, 1)))
        return red, black

    for yb in range(3):
        row_ok = (up_in, True, down_in)[yb]
        ok = ring_in & row_ok

        def spread1(r, carry, yb=yb, ok=ok):
            red, black = apart(joined(KX, yb, r))
            K1[0, 8 * yb + r] = jnp.where(ok, red, 0.0)
            K1[1, 8 * yb + r] = jnp.where(ok, black, 0.0)
            return carry

        lax.fori_loop(0, 8, spread1, 0)
        for r in range(4):
            red, black = apart(joined(KX, yb, 8 + r))
            K2[0, 1 + 4 * yb + r] = jnp.where(ok, red, 0.0)
            K2[1, 1 + 4 * yb + r] = jnp.where(ok, black, 0.0)

    def near_y(level, ref, c, r):
        dx, dz = (1, 2) if level == 1 else (2, 4)
        p = parity_y(level, lane2, sub2)
        o, low, high = ref[1 - c, r], ref[1 - c, r - 1], ref[1 - c, r + 1]
        outer = jnp.where(p, high, low) if c == 0 else jnp.where(p, low, high)
        ahead, behind = ring(o, dz)
        return (o, outer, roll(o, -dx, 0), roll(o, dx, 0), ahead, behind)

    def faces_y(level, K, G, I, D, r):
        dx = 1 if level == 1 else 2
        s = 0.25**level
        for c in range(2):
            k = K[c, r]
            near = list(near_y(level, K, c, r))
            last, first = sub2 >= 8 - dx, sub2 < dx
            near[2] = jnp.where(last, 0.0, near[2])
            near[3] = jnp.where(first, 0.0, near[3])
            f = [0.5 * (k + value) for value in near]
            d = ((f[0] + f[1]) + (f[2] + f[3])) + (f[4] + f[5])
            inv = jnp.where(k > 0.0, 1.0 / d, 0.0)
            for n in range(6):
                g = f[n] * inv
                if n == 2:
                    g = jnp.where(last, 0.0, g)
                if n == 3:
                    g = jnp.where(first, 0.0, g)
                G[c, r, n] = g
            I[c, r] = inv * (1.0 / s)
            if c == 0:
                D[r] = s * d

    loop(2, R1 - 2, lambda r, j: faces_y(1, K1, G1, I1, D1, r))
    loop(1, R2 - 1, lambda r, j: faces_y(2, K2, G2, I2, D2, r))

    all_bytes(GK, gr.at[0])
    k3r, k3b = global_level3(GK)
    row3 = lax.broadcasted_iota(jnp.int32, (64, 128), 0)
    lane3 = lax.broadcasted_iota(jnp.int32, (64, 128), 1)
    odd3 = (row3 + lane3) % 2 == 1
    edges3 = (row3 == 0, row3 == 63, lane3 == 0, lane3 == 127)

    def near3(o):
        return (roll(o, 1, 0), roll(o, -1, 0), roll(o, 1, 1), roll(o, -1, 1), o)

    def faces3(c, k, o):
        s = 0.25**3
        near = [jnp.where(e, 0.0, v) for e, v in zip(edges3, near3(o))] + [o]
        f = [0.5 * (k + value) for value in near] + [0.5 * k]
        d = ((f[0] + f[1]) + (f[2] + f[3])) + (f[4] + f[5])
        inv = 1.0 / d
        for n in range(5):
            g = f[n] * inv
            G3[c, n] = jnp.where(edges3[n], 0.0, g) if n < 4 else g
        I3[c] = inv * (1.0 / s)
        if c == 0:
            D3[...] = s * d

    faces3(0, k3r, k3b)
    faces3(1, k3b, k3r)

    lane4 = lax.broadcasted_iota(jnp.int32, (16, 128), 1)
    row4 = lax.broadcasted_iota(jnp.int32, (16, 128), 0)
    p4 = (lane4 // 2) % 2 == 1

    def level4_of(total):
        t = total + swap_subs(total, 1)
        buf4[...] = 0.125 * (t + swap_lanes(t, 1))
        low, high = buf4[pl.ds(0, 16, stride=4), :], buf4[pl.ds(2, 16, stride=4), :]
        return split(p4, low, high)

    k4 = level4_of(k3r + k3b)

    def near4(c, o):
        low, high = roll(o, 1, 0), roll(o, -1, 0)
        outer = jnp.where(p4, high, low) if c == 0 else jnp.where(p4, low, high)
        return (o, outer, roll(o, -2, 1), roll(o, 2, 1))

    def faces4(c):
        s = 0.25**4
        k = k4[c]
        take = p4 if c == 0 else jnp.logical_not(p4)
        edges = (None, jnp.where(take, row4, 15 - row4) == 15, lane4 >= 126, lane4 < 2)
        near = near4(c, k4[1 - c])
        near = [v if e is None else jnp.where(e, 0.0, v) for e, v in zip(edges, near)]
        f = [0.5 * (k + value) for value in near]
        d = ((f[0] + f[1]) + (f[2] + f[3])) + k
        inv = 1.0 / d
        g = [v * inv if e is None else jnp.where(e, 0.0, v * inv) for e, v in zip(edges, f)]
        return g, inv * (1.0 / s)

    g4r, i4r = faces4(0)
    g4b, i4b = faces4(1)

    received(x_b1)

    def v0_pieces(dy, dz):
        def at(r, n):
            return V0.at[1, pl.ds(r, n), :, pl.ds(0, 128)]

        lo, n, to = {-1: (HY, 5, HY + NY), 0: (HY, NY, HY), 1: (HY + NY - 5, 5, HY - 5)}[dy]
        if dz == 0:
            return at(lo, n), at(to, n)
        return at(lo, n), zv.at[0 if dz > 0 else 1, pl.ds(to, n)]

    x_v0 = exchange(X_V0, v0_pieces)

    for yb in range(3):

        def spread_b(r, carry, yb=yb):
            red, black = apart(joined(BX, yb, r))
            row = 8 * yb + r
            BD1[0, row] = red * I1[0, row]
            BD1[1, row] = black * I1[1, row]
            V1[0, row] = red * I1[0, row]
            return carry

        lo, hi = ((2, 8), (0, 8), (0, 6))[yb]
        lax.fori_loop(lo, hi, spread_b, 0)

    def update_y(level, V, G, BD, c, r):
        near = near_y(level, V, c, r)
        t = [G[c, r, n] * near[n] for n in range(6)]
        return BD[c, r] + (((t[0] + t[1]) + (t[2] + t[3])) + (t[4] + t[5]))

    def sweep_y(level, V, G, BD, c, lo, hi):
        def body(r, j):
            V[c, r] = update_y(level, V, G, BD, c, r)

        loop(lo, hi, body)

    sweep_y(1, V1, G1, BD1, 1, 2, 22)
    sweep_y(1, V1, G1, BD1, 0, 2, 22)
    sweep_y(1, V1, G1, BD1, 1, 2, 22)

    p2w = parity_y(2, lane2, sub2)

    def right2(i, carry):
        rows = []
        for j in range(2):
            r = 4 + 2 * i + j
            t = D1[r] * (update_y(1, V1, G1, BD1, 0, r) - V1[0, r])
            t = t + swap_subs(t, 1)
            a, b = t[:, :128], t[:, 128:]
            rows.append(0.125 * cat(a + swap_lanes(a, 2), b + swap_lanes(b, 2)))
        red, black = split(p2w, rows[0], rows[1])
        row = 3 + i
        BD2[0, row] = red * I2[0, row]
        BD2[1, row] = black * I2[1, row]
        V2[0, row] = red * I2[0, row]
        pair2[i] = jnp.where(odd, black[:, :128], red[:, :128])
        return carry

    V2[0, 2] = zero_row
    V2[0, 11] = zero_row
    V2[1, 2] = zero_row
    V2[1, 11] = zero_row
    lax.fori_loop(0, 8, right2, 0)

    sweep_y(2, V2, G2, BD2, 1, 3, 11)
    sweep_y(2, V2, G2, BD2, 0, 3, 11)
    sweep_y(2, V2, G2, BD2, 1, 3, 11)
    rows = []
    for y in range(4):
        r = 5 + y
        t = (D2[r] * (update_y(2, V2, G2, BD2, 0, r) - V2[0, r]))[:, :128]
        t = t + swap_subs(t, 2)
        rows.append(0.125 * (t + swap_lanes(t, 4)))
    gather(msg_b, GB, 1, message(rows))

    for y in range(4):
        CX[1, 1, y] = jnp.where(lane % 4 < 2, pair2[2 + y], V2[1, 5 + y, :, :128])
    x_b2 = exchange(X_B2, block_pieces(CX))
    received(x_v0)
    for copy in x_v0:
        copy.wait_send()

    def v0_sides(r, j):
        ok = ((r >= HY) | up_in) & ((r < HY + NY) | down_in)
        V0[1, r, :, 128:] = jnp.where(
            ok & (((lane < 5) & right_in) | ((lane >= 123) & left_in)), jnp.where(lane < 64, zv[1, r], zv[0, r]), 0.0
        )
        V0[1, r, :, :128] = jnp.where(ok, V0[1, r, :, :128], 0.0)

    loop(HY - 5, HY + NY + 5, v0_sides)
    received(x_b2)
    for yb in range(3):
        row_ok = (up_in, True, down_in)[yb]
        for r in range(4):
            x = joined(CX, yb, r)
            row = 1 + 4 * yb + r

            def fill(x):
                a, b = x[:, :128], x[:, 128:]
                first = cat(jnp.where(odd, roll(a, 1, 1), a), jnp.where(odd, roll(b, 1, 1), b))
                second = cat(jnp.where(odd, a, roll(a, -1, 1)), jnp.where(odd, b, roll(b, -1, 1)))
                return first, second

            first, second = fill(x)
            head = lane2 % 4 < 2

            def pair_up(y):
                return cat(roll(y[:, :128], 2, 1), roll(y[:, 128:], 2, 1))

            def pair_down(y):
                return cat(roll(y[:, :128], -2, 1), roll(y[:, 128:], -2, 1))

            BD2[0, row] = jnp.where(head, first, pair_up(first)) * I2[0, row]
            BD2[1, row] = jnp.where(head, second, pair_up(second)) * I2[1, row]
            V2[1, row] = jnp.where(ring_in & row_ok, jnp.where(head, pair_down(x), x), 0.0)

    zrow = lax.broadcasted_iota(jnp.int32, (128, 256), 0)
    zcol = lax.broadcasted_iota(jnp.int32, (128, 256), 1)
    expand = (zrow == gz * 16 + zcol // 8 - jnp.where(zcol >= 192, 32, 0)).astype(F32)

    all_bytes(GB, gr.at[1])
    b3r, b3b = global_level3(GB)
    bd3 = (b3r * I3[0], b3b * I3[1])

    def update3(c, o):
        near = near3(o)
        t = [G3[c, n] * near[n] for n in range(5)]
        return bd3[c] + (((t[0] + t[1]) + (t[2] + t[3])) + t[4])

    v_r = bd3[0]
    v_b = update3(1, v_r)
    v_r = update3(0, v_b)
    v_b = update3(1, v_r)
    r3 = D3[...] * (update3(0, v_b) - v_r)
    b4 = level4_of(r3)
    bd4r, bd4b = b4[0] * i4r, b4[1] * i4b

    def update4(c, g, bd, o):
        near = near4(c, o)
        return bd + ((g[0] * near[0] + g[1] * near[1]) + (g[2] * near[2] + g[3] * near[3]))

    def sweep4(i, carry):
        red, black = carry
        red = update4(0, g4r, bd4r, black)
        black = update4(1, g4b, bd4b, red)
        return red, black

    zero4 = jnp.zeros((16, 128), F32)
    e_r, e_b = lax.fori_loop(0, COARSE_SWEEPS, sweep4, (zero4, zero4))
    low, high = split(p4, e_r, e_b)
    buf4[pl.ds(0, 16, stride=4), :] = low
    buf4[pl.ds(1, 16, stride=4), :] = low
    buf4[pl.ds(2, 16, stride=4), :] = high
    buf4[pl.ds(3, 16, stride=4), :] = high
    v_b = v_b + buf4[...]
    v_r = update3(0, v_b)
    v_b = update3(1, v_r)
    v_r = update3(0, v_b)
    v_b = update3(1, v_r)

    x_low, x_high = split(odd3, v_r, v_b)
    e3x[0, pl.ds(8, 64), :] = x_low
    e3x[1, pl.ds(8, 64), :] = x_high
    parts = []
    for n in range(2):
        for i in range(12):
            parts.append(e3x[n, pl.ds(gy * 4 + (4 + i), 1), :])
    wide = dot(jnp.concatenate(parts, axis=0), expand)
    for i in range(12):
        e = jnp.where(sub2 < 4, wide[i : i + 1], wide[12 + i : 13 + i])
        row_ok = up_in if i < 4 else (down_in if i >= 8 else True)
        V2[1, 1 + i] = V2[1, 1 + i] + jnp.where(ring_in & row_ok, e, 0.0)
    sweep_y(2, V2, G2, BD2, 0, 1, 13)
    sweep_y(2, V2, G2, BD2, 1, 1, 13)
    sweep_y(2, V2, G2, BD2, 0, 1, 13)
    sweep_y(2, V2, G2, BD2, 1, 3, 11)

    p1w = parity_y(1, lane2, sub2)

    def correct1(i, carry):
        low, high = split(p2w, V2[0, 3 + i], V2[1, 3 + i])
        V1[1, 4 + 2 * i] = V1[1, 4 + 2 * i] + low
        V1[1, 5 + 2 * i] = V1[1, 5 + 2 * i] + high
        return carry

    lax.fori_loop(0, 8, correct1, 0)
    sweep_y(1, V1, G1, BD1, 0, 4, 20)
    sweep_y(1, V1, G1, BD1, 1, 4, 20)
    sweep_y(1, V1, G1, BD1, 0, 4, 20)
    sweep_y(1, V1, G1, BD1, 1, 6, 18)

    def correct0(i, carry):
        low, high = split(p1w, V1[0, 6 + i], V1[1, 6 + i])
        for j in range(2):
            V0[1, 4 * i + j] = V0[1, 4 * i + j] + low
            V0[1, 4 * i + 2 + j] = V0[1, 4 * i + 2 + j] + high
        return carry

    lax.fori_loop(0, 12, correct0, 0)
    sweep0(0, 4, R0 - 4)
    sweep0(1, 4, R0 - 4)
    sweep0(0, 6, R0 - 6)
    sweep0(1, 6, R0 - 6)

    def results(r, j):
        y = r - HY
        par = odd if j % 2 == 0 else jnp.logical_not(odd)

        def put(n, red, black):
            tmp[n, pl.ds(y, 8, stride=2 * NY), :] = jnp.where(par, black, red)
            tmp[n, pl.ds(NY + y, 8, stride=2 * NY), :] = jnp.where(par, red, black)

        v_red, v_black = V0[0, r], V0[1, r]
        put(0, v_red[:, :128], v_black[:, :128])
        res_red = D0[0, r] * (update0(0, r, j) - v_red)
        res_black = D0[1, r] * (update0(1, r, j) - v_black)
        put(1, res_red[:, :128], res_black[:, :128])
        put(2, und[0, r, :, :128], und[1, r, :, :128])

    loop(HY, HY + NY, results)
    for x in range(NX):
        outb[x] = tmp[2, pl.ds(x * NY, NY), :].astype(BF16)
        pb[0, x] = tmp[0, pl.ds(x * NY, NY), :]
        pb[1, x] = tmp[1, pl.ds(x * NY, NY), :]
    stores = []
    for n, (src, dst) in enumerate(((outb, phase_o), (pb.at[0], pres_o), (pb.at[1], res_o))):
        copy = pltpu.make_async_copy(src, dst, osem.at[n])
        copy.start()
        stores.append(copy)

    for copies in (x_in, x_f, x_k, x_b1, x_b2):
        for copy in copies:
            copy.wait_send()
    all_bytes(GK, gs.at[0])
    all_bytes(GB, gs.at[1])
    for copy in stores:
        copy.wait()


def per_device(GY, GZ, phase, undercool, perm_base, source, pressure):
    def vm(*shape):
        return pltpu.VMEM(shape, F32)

    scratch = [
        pltpu.VMEM((3, NX, NY, NZ), BF16),
        vm(2, NX, NY, NZ),
        vm(5, NX * NY, NZ),
        vm(2, NX, NY, NZ),
        pltpu.VMEM((NX, NY, NZ), BF16),
        pltpu.VMEM((R0, 48, 128), BF16),
        vm(R0, 24, 128),
        pltpu.VMEM((4, 48, 128), BF16),
        vm(4, 24, 128),
        pltpu.VMEM((2, 6, 48, 128), BF16),
        vm(2, 6, 24, 128),
        vm(2, R0, 8, 256),
        vm(2, R0, 8, 256),
        vm(2, R0, 8, 256),
        vm(2, R0, 8, 256),
        vm(2, R0, 8, 256),
        vm(2, R0, 8, 256),
        vm(2, R0, 6, 8, 256),
        vm(2, R0, 8, 256),
        vm(2, R0, 8, 256),
        vm(2, R0, 8, 128),
        vm(3, 3, 12, 8, 128),
        vm(3, 3, 8, 8, 128),
        vm(3, 3, 4, 8, 128),
        vm(2, R1, 8, 256),
        vm(2, R1, 8, 256),
        vm(2, R1, 6, 8, 256),
        vm(2, R1, 8, 256),
        vm(2, R1, 8, 256),
        vm(R1, 8, 256),
        vm(2, R2, 8, 256),
        vm(2, R2, 8, 256),
        vm(2, R2, 6, 8, 256),
        vm(2, R2, 8, 256),
        vm(2, R2, 8, 256),
        vm(R2, 8, 256),
        vm(1, 1, 128),
        vm(1, 1, 128),
        vm(GY * GZ, 1, 128),
        vm(GY * GZ, 1, 128),
        vm(2, 64, 128),
        vm(2, 5, 64, 128),
        vm(2, 64, 128),
        vm(64, 128),
        vm(64, 128),
        vm(2, 80, 128),
        vm(8, 8, 128),
        pltpu.SemaphoreType.DMA((N_X, 8)),
        pltpu.SemaphoreType.DMA((N_X, 8)),
        pltpu.SemaphoreType.DMA((2,)),
        pltpu.SemaphoreType.DMA((2,)),
        pltpu.SemaphoreType.DMA((5,)),
        pltpu.SemaphoreType.DMA((3,)),
    ]
    hbm = pl.BlockSpec(memory_space=pl.ANY)
    return pl.pallas_call(
        functools.partial(kernel, GY, GZ),
        out_shape=(
            jax.ShapeDtypeStruct((NX, NY, NZ), BF16),
            jax.ShapeDtypeStruct((NX, NY, NZ), F32),
            jax.ShapeDtypeStruct((NX, NY, NZ), F32),
        ),
        in_specs=[hbm] * 5,
        out_specs=(hbm, hbm, hbm),
        scratch_shapes=scratch,
        compiler_params=pltpu.CompilerParams(
            collective_id=0, has_side_effects=True, vmem_limit_bytes=48 * 2**20
        ),
    )(phase, undercool, perm_base, source, pressure)


def solution(mesh):
    spec = P(None, "gy", "gz")
    return jax.shard_map(
        functools.partial(per_device, mesh.shape["gy"], mesh.shape["gz"]),
        mesh=mesh,
        in_specs=(spec,) * 5,
        out_specs=(spec,) * 3,
        check_vma=False,
    )
```

time: 1800 us -> 80.4 us (0.04); the launches traced: 1770 us -> 80.1 us
  starting transfers between devices: 1120 us -> 0 us
  other arithmetic: 257 us -> 0 us
  local copies, waits for them, and re-layouts: 213 us -> 6.67 us
  waiting for transfers between devices: 180 us -> 0 us
  Pallas kernels: 0 us -> 72.8 us
    ppermute x332 -> x0, starting transfers between devices: 1120 us -> none  [the longest x166 843 us: extended(): before = lax.ppermute(last, axis, up)]
    ppermute x332 -> x0, waiting for transfers between devices: 180 us -> none  [the longest x166 133 us: extended(): after = lax.ppermute(initial, axis, down)]
    select_n x72 -> x0, other arithmetic: 99.5 us -> none  [half_sweep(): return jnp.where(red_cells, update, iterate)]
    concatenate x224 -> x0, other arithmetic: 89.4 us -> none  [extended(): shard = jnp.concatenate([before, shard, after], axis=dim)]
    slice x173 -> x0, local copies, waits for them, and re-layouts: 76.9 us -> none  [the longest x111 55.5 us: extended(): last = lax.slice_in_dim(shard, length - width, length, axis=dim)]
    pallas_call x0 -> x1, Pallas kernels: none -> 72.8 us  [per_device(): pl.pallas_call(functools.partial(kernel, GY, GZ), out_shape=(jax.ShapeDty...]
    reshape x9 -> x0, local copies, waits for them, and re-layouts: 49.4 us -> none  [the longest x4 42.1 us: restrict(): blocks = array.reshape(n_one // 2, 2, n_two // 2, 2, n_three // 2, 2)]
    ppermute x22 -> x0, local copies, waits for them, and re-layouts: 32.2 us -> none  [the longest x11 16.3 us: extended(): before = lax.ppermute(last, axis, up)]
  transfers between devices with their start and end apart: 332 -> 0, of which waited for: 117 -> 0; matrix products, arithmetic and copies ran while one was open for 10% -> 0% of each run, Pallas kernels for 0% -> 0%
where the time goes in v1:
time: 80.4 us; the launch traced here: 80.1 us
  Pallas kernels  72.8 us (91%)
  local copies, waits for them, and re-layouts  6.67 us (8%)
    pallas_call x1, Pallas kernels, per_device(): pl.pallas_call(functools.partial(kernel, GY, GZ), out_shape=(jax.ShapeDty...  72.8 us
    unnamed x13, local copies, waits for them, and re-layouts  6.67 us

profile of v1, /device:TPU:1, one launch (start us, length us, event | category | flops | bytes accessed | tf_op | source)
XLA Modules:
  0.0 80.1 jit_solution(10543749787231138676)
XLA Ops:
  0.6 0.0 copy-start
  0.6 0.9 %copy-done = f32[16,32,128]{2,1,0:T(8,128)S(1)} copy-done((f32[16,32,128]{2,1,0:T(8,128)S(1)}, f32[16,32,128]{2,1,0:T(8,128)}, u32[]{:S(2)}) %copy-start) | copy-done | bytes 262168
  1.6 0.0 copy-start.1
  1.6 0.9 %copy-done.1 = f32[16,32,128]{2,1,0:T(8,128)S(1)} copy-done((f32[16,32,128]{2,1,0:T(8,128)S(1)}, f32[16,32,128]{2,1,0:T(8,128)}, u32[]{:S(2)}) %copy-start.1) | copy-done | bytes 262168
  2.5 0.0 copy-start.2
  2.5 0.9 %copy-done.2 = bf16[16,32,128]{2,1,0:T(8,128)(2,1)S(1)} copy-done((bf16[16,32,128]{2,1,0:T(8,128)(2,1)S(1)}, bf16[16,32,128]{2,1,0:T(8,128)(2,1)}, u32[]{:S(2)}) %copy-start.2) | copy-done | bytes 131096
  3.4 0.0 copy-start.3
  3.4 0.9 %copy-done.3 = bf16[16,32,128]{2,1,0:T(8,128)(2,1)S(1)} copy-done((bf16[16,32,128]{2,1,0:T(8,128)(2,1)S(1)}, bf16[16,32,128]{2,1,0:T(8,128)(2,1)}, u32[]{:S(2)}) %copy-start.3) | copy-done | bytes 131096
  4.3 0.0 copy-start.4
  4.3 0.9 %copy-done.4 = bf16[16,32,128]{2,1,0:T(8,128)(2,1)S(1)} copy-done((bf16[16,32,128]{2,1,0:T(8,128)(2,1)S(1)}, bf16[16,32,128]{2,1,0:T(8,128)(2,1)}, u32[]{:S(2)}) %copy-start.4) | copy-done | bytes 131096
  5.2 72.8 %shard_map.76 = (bf16[16,32,128]{2,1,0:T(8,128)(2,1)S(1)}, f32[16,32,128]{2,1,0:T(8,128)S(1)}, f32[16,32,128]{2,1,0:T(8,128)S(1)}) custom-call(bf16[16,32,128]{2,1,0:T(8,128)(2,1)S(1)} %copy-done.2, bf16[16,32,128]{2,1,0:T(8,128)(2,1)S(1)} %copy-done.3, bf16[16,32,128]{2,1,0:T(8,128)(2,1)S(1)} %copy-done.4, f32[16,32,128]{2,1,0:T(8,128)S(1)} %copy-done, ...), custom_call_target="tpu_custom_call" | custom-call | tf_op jit(solution)/shard_map/pallas_call | solution.py:815
  78.1 0.7 copy.11
  78.7 0.7 copy.12
  79.4 0.7 copy.13
Async XLA Ops:
  0.6 1.0 %copy-start = (f32[16,32,128]{2,1,0:T(8,128)S(1)}, f32[16,32,128]{2,1,0:T(8,128)}, u32[]{:S(2)}) copy-start(f32[16,32,128]{2,1,0:T(8,128)} %src_h.1) | copy-start | bytes 786436
  1.6 0.9 %copy-start.1 = (f32[16,32,128]{2,1,0:T(8,128)S(1)}, f32[16,32,128]{2,1,0:T(8,128)}, u32[]{:S(2)}) copy-start(f32[16,32,128]{2,1,0:T(8,128)} %pres_h.1) | copy-start | bytes 786436
  2.5 0.9 %copy-start.2 = (bf16[16,32,128]{2,1,0:T(8,128)(2,1)S(1)}, bf16[16,32,128]{2,1,0:T(8,128)(2,1)}, u32[]{:S(2)}) copy-start(bf16[16,32,128]{2,1,0:T(8,128)(2,1)} %phase_h.1) | copy-start | bytes 393220
  3.4 0.9 %copy-start.3 = (bf16[16,32,128]{2,1,0:T(8,128)(2,1)S(1)}, bf16[16,32,128]{2,1,0:T(8,128)(2,1)}, u32[]{:S(2)}) copy-start(bf16[16,32,128]{2,1,0:T(8,128)(2,1)} %under_h.1) | copy-start | bytes 393220
  4.3 0.9 %copy-start.4 = (bf16[16,32,128]{2,1,0:T(8,128)(2,1)S(1)}, bf16[16,32,128]{2,1,0:T(8,128)(2,1)}, u32[]{:S(2)}) copy-start(bf16[16,32,128]{2,1,0:T(8,128)(2,1)} %perm_h.1) | copy-start | bytes 393220

commit v2 on v1

--- a/solution.py
+++ b/solution.py
@@ -28,11 +28,19 @@
 
 def loop(lo, hi, body, step=2):
     def trip(i, carry):
+        stores = []
         for j in range(step):
-            body(lo + i * step + j, j)
+            stores.extend(body(lo + i * step + j, j))
+        for ref, index, value in stores:
+            ref[index] = value
         return carry
 
-    lax.fori_loop(0, (hi - lo) // step, trip, 0)
+    trips = (hi - lo) // step
+    assert trips * step == hi - lo
+    if trips == 1:
+        trip(0, 0)
+    else:
+        lax.fori_loop(0, trips, trip, 0)
 
 
 def kernel(
@@ -40,8 +48,8 @@
     inb, inf, tmp, pb, outb,
     ha, hf, zp, zpf, zb, zbf,
     ice, und, prm, S0, V0, K0, G0, BD0, D0, zv,
-    KX, BX, CX, K1, V1, G1, I1, BD1, D1, K2, V2, G2, I2, BD2, D2,
-    msg_k, msg_b, GK, GB, K3, G3, I3, D3, buf4, e3x, pair2,
+    KX, CX, K1, V1, G1, I1, BD1, D1, K2, V2, G2, I2, BD2, D2,
+    b1, zp1, zb1, msg_k, msg_b, GK, GB, K3, G3, I3, D3, buf4, e3x, pair2,
     ssem, rsem, gs, gr, lsem, osem,
 ):
     gy, gz = lax.axis_index("gy"), lax.axis_index("gz")
@@ -229,6 +237,7 @@
         return (ref[1 - c, r - 1], ref[1 - c, r + 1], o, x_outer(o, take), ahead, behind)
 
     def permeability(r, j):
+        stores = []
         for c in range(2):
             now = ice[c, r]
             near = list(near0(ice, c, r, j))
@@ -240,8 +249,9 @@
             well = 2.0 * now * (1.0 - now) * (1.0 - 2.0 * now)
             drive = 30.0 * now * now * (1.0 - now) * (1.0 - now) * und[c, r]
             new = jnp.clip(now + 0.12 * lap - 0.5 * well + 0.25 * drive, 0.0, 1.0)
-            K0[c, r] = jnp.where(prm[c, r] > 0.0, prm[c, r] * jnp.exp(-1.5 * new), 0.0)
-            und[c, r] = new
+            stores.append((K0, (c, r), jnp.where(prm[c, r] > 0.0, prm[c, r] * jnp.exp(-1.5 * new), 0.0)))
+            stores.append((und, (c, r), new))
+        return stores
 
     loop(2, R0 - 2, permeability)
 
@@ -340,6 +350,7 @@
     gather(msg_k, GK, 0, message(k3_rows))
 
     def faces0(r, j):
+        stores = []
         ok = row_mask(r, 5)
         for c in range(2):
             k = K0[c, r]
@@ -352,9 +363,10 @@
             inv = jnp.where(ok, 1.0 / d, 0.0)
             for n in range(6):
                 g = f[n] * inv
-                G0[c, r, n] = jnp.where(edge, 0.0, g) if n == 3 else g
-            BD0[c, r] = jnp.where(ok, S0[c, r], 0.0) * inv
-            D0[c, r] = d
+                stores.append((G0, (c, r, n), jnp.where(edge, 0.0, g) if n == 3 else g))
+            stores.append((BD0, (c, r), jnp.where(ok, S0[c, r], 0.0) * inv))
+            stores.append((D0, (c, r), d))
+        return stores
 
     loop(4, R0 - 4, faces0)
 
@@ -365,9 +377,9 @@
 
     def sweep0(c, lo, hi):
         def body(r, j):
-            V0[c, r] = update0(c, r, j)
-
-        loop(lo, hi, body)
+            return [(V0, (c, r), update0(c, r, j % 2))]
+
+        loop(lo, hi, body, 4)
 
     sweep0(0, 4, R0 - 4)
     sweep0(1, 4, R0 - 4)
@@ -377,18 +389,33 @@
     def defect0(r, j):
         return (D0[0, r] * (update0(0, r, j) - V0[0, r]))[:, :128]
 
-    def right1(yp, carry):
+    def right1(yp, j):
         rows = []
         for j in range(2):
             r = HY + 4 * yp + 2 * j
             t = defect0(r, 0) + defect0(r + 1, 1)
             rows.append(0.125 * (t + swap_lanes(t, 1)))
         red, black = split(p1, rows[0], rows[1])
-        BX[1, 1, yp] = jnp.where(odd, black, red)
-        return carry
-
-    lax.fori_loop(0, 8, right1, 0)
-    x_b1 = exchange(X_B1, block_pieces(BX))
+        return [(b1, (8 + yp,), jnp.where(odd, black, red))]
+
+    loop(0, 8, right1, 2)
+    for k in range(4):
+        first, second = b1[8 + 2 * k], b1[9 + 2 * k]
+        zp1[k] = jnp.where(lane < 64, roll(first, 32, 1), roll(second, 96, 1))
+
+    def b1_pieces(dy, dz):
+        if dz == 0 and dy < 0:
+            return b1.at[pl.ds(8, 6)], b1.at[pl.ds(16, 6)]
+        if dz == 0:
+            return b1.at[pl.ds(10, 6)], b1.at[pl.ds(2, 6)]
+        side = 0 if dz > 0 else 1
+        if dy == 0:
+            return zp1, zb1.at[side, pl.ds(4, 4)]
+        if dy > 0:
+            return zp1.at[pl.ds(1, 3)], zb1.at[side, pl.ds(1, 3)]
+        return zp1.at[pl.ds(0, 3)], zb1.at[side, pl.ds(8, 3)]
+
+    x_b1 = exchange(X_B1, b1_pieces)
 
     received(x_k)
 
@@ -430,6 +457,7 @@
     def faces_y(level, K, G, I, D, r):
         dx = 1 if level == 1 else 2
         s = 0.25**level
+        stores = []
         for c in range(2):
             k = K[c, r]
             near = list(near_y(level, K, c, r))
@@ -445,10 +473,11 @@
                     g = jnp.where(last, 0.0, g)
                 if n == 3:
                     g = jnp.where(first, 0.0, g)
-                G[c, r, n] = g
-            I[c, r] = inv * (1.0 / s)
+                stores.append((G, (c, r, n), g))
+            stores.append((I, (c, r), inv * (1.0 / s)))
             if c == 0:
-                D[r] = s * d
+                stores.append((D, (r,), s * d))
+        return stores
 
     loop(2, R1 - 2, lambda r, j: faces_y(1, K1, G1, I1, D1, r))
     loop(1, R2 - 1, lambda r, j: faces_y(2, K2, G2, I2, D2, r))
@@ -523,20 +552,18 @@
             return at(lo, n), at(to, n)
         return at(lo, n), zv.at[0 if dz > 0 else 1, pl.ds(to, n)]
 
-    x_v0 = exchange(X_V0, v0_pieces)
-
-    for yb in range(3):
-
-        def spread_b(r, carry, yb=yb):
-            red, black = apart(joined(BX, yb, r))
-            row = 8 * yb + r
-            BD1[0, row] = red * I1[0, row]
-            BD1[1, row] = black * I1[1, row]
-            V1[0, row] = red * I1[0, row]
-            return carry
-
-        lo, hi = ((2, 8), (0, 8), (0, 6))[yb]
-        lax.fori_loop(lo, hi, spread_b, 0)
+    def spread_b(k, j):
+        stores = []
+        merged = jnp.where(lane % 64 < 32, zb1[0, k], zb1[1, k])
+        for q in range(2):
+            r = 2 * k + q
+            red, black = apart(cat(b1[r], roll(merged, -64 * q - 32, 1)))
+            stores.append((BD1, (0, r), jnp.where(I1[0, r] > 0.0, red, 0.0) * I1[0, r]))
+            stores.append((BD1, (1, r), jnp.where(I1[1, r] > 0.0, black, 0.0) * I1[1, r]))
+            stores.append((V1, (0, r), stores[-2][2]))
+        return stores
+
+    loop(1, 11, spread_b, 2)
 
     def update_y(level, V, G, BD, c, r):
         near = near_y(level, V, c, r)
@@ -545,9 +572,9 @@
 
     def sweep_y(level, V, G, BD, c, lo, hi):
         def body(r, j):
-            V[c, r] = update_y(level, V, G, BD, c, r)
-
-        loop(lo, hi, body)
+            return [(V, (c, r), update_y(level, V, G, BD, c, r))]
+
+        loop(lo, hi, body, 4)
 
     sweep_y(1, V1, G1, BD1, 1, 2, 22)
     sweep_y(1, V1, G1, BD1, 0, 2, 22)
@@ -555,7 +582,7 @@
 
     p2w = parity_y(2, lane2, sub2)
 
-    def right2(i, carry):
+    def right2(i, j):
         rows = []
         for j in range(2):
             r = 4 + 2 * i + j
@@ -565,17 +592,19 @@
             rows.append(0.125 * cat(a + swap_lanes(a, 2), b + swap_lanes(b, 2)))
         red, black = split(p2w, rows[0], rows[1])
         row = 3 + i
-        BD2[0, row] = red * I2[0, row]
-        BD2[1, row] = black * I2[1, row]
-        V2[0, row] = red * I2[0, row]
-        pair2[i] = jnp.where(odd, black[:, :128], red[:, :128])
-        return carry
+        first = red * I2[0, row]
+        return [
+            (BD2, (0, row), first),
+            (V2, (0, row), first),
+            (BD2, (1, row), black * I2[1, row]),
+            (pair2, (i,), jnp.where(odd, black[:, :128], red[:, :128])),
+        ]
 
     V2[0, 2] = zero_row
     V2[0, 11] = zero_row
     V2[1, 2] = zero_row
     V2[1, 11] = zero_row
-    lax.fori_loop(0, 8, right2, 0)
+    loop(0, 8, right2, 2)
 
     sweep_y(2, V2, G2, BD2, 1, 3, 11)
     sweep_y(2, V2, G2, BD2, 0, 3, 11)
@@ -591,18 +620,7 @@
     for y in range(4):
         CX[1, 1, y] = jnp.where(lane % 4 < 2, pair2[2 + y], V2[1, 5 + y, :, :128])
     x_b2 = exchange(X_B2, block_pieces(CX))
-    received(x_v0)
-    for copy in x_v0:
-        copy.wait_send()
-
-    def v0_sides(r, j):
-        ok = ((r >= HY) | up_in) & ((r < HY + NY) | down_in)
-        V0[1, r, :, 128:] = jnp.where(
-            ok & (((lane < 5) & right_in) | ((lane >= 123) & left_in)), jnp.where(lane < 64, zv[1, r], zv[0, r]), 0.0
-        )
-        V0[1, r, :, :128] = jnp.where(ok, V0[1, r, :, :128], 0.0)
-
-    loop(HY - 5, HY + NY + 5, v0_sides)
+    x_v0 = exchange(X_V0, v0_pieces)
     received(x_b2)
     for yb in range(3):
         row_ok = (up_in, True, down_in)[yb]
@@ -629,6 +647,18 @@
             BD2[1, row] = jnp.where(head, second, pair_up(second)) * I2[1, row]
             V2[1, row] = jnp.where(ring_in & row_ok, jnp.where(head, pair_down(x), x), 0.0)
 
+    received(x_v0)
+    for copy in x_v0:
+        copy.wait_send()
+
+    def v0_sides(r, j):
+        ok = ((r >= HY) | up_in) & ((r < HY + NY) | down_in)
+        side = jnp.where(
+            ok & (((lane < 5) & right_in) | ((lane >= 123) & left_in)), jnp.where(lane < 64, zv[1, r], zv[0, r]), 0.0
+        )
+        return [(V0, (1, r), cat(jnp.where(ok, V0[1, r, :, :128], 0.0), side))]
+
+    loop(HY - 5, HY + NY + 5, v0_sides, 3)
     zrow = lax.broadcasted_iota(jnp.int32, (128, 256), 0)
     zcol = lax.broadcasted_iota(jnp.int32, (128, 256), 1)
     expand = (zrow == gz * 16 + zcol // 8 - jnp.where(zcol >= 192, 32, 0)).astype(F32)
@@ -692,26 +722,23 @@
 
     p1w = parity_y(1, lane2, sub2)
 
-    def correct1(i, carry):
+    def correct1(i, j):
         low, high = split(p2w, V2[0, 3 + i], V2[1, 3 + i])
-        V1[1, 4 + 2 * i] = V1[1, 4 + 2 * i] + low
-        V1[1, 5 + 2 * i] = V1[1, 5 + 2 * i] + high
-        return carry
-
-    lax.fori_loop(0, 8, correct1, 0)
+        return [(V1, (1, 4 + 2 * i + n), V1[1, 4 + 2 * i + n] + e) for n, e in ((0, low), (1, high))]
+
+    loop(0, 8, correct1, 4)
     sweep_y(1, V1, G1, BD1, 0, 4, 20)
     sweep_y(1, V1, G1, BD1, 1, 4, 20)
     sweep_y(1, V1, G1, BD1, 0, 4, 20)
     sweep_y(1, V1, G1, BD1, 1, 6, 18)
 
-    def correct0(i, carry):
+    def correct0(i, j):
         low, high = split(p1w, V1[0, 6 + i], V1[1, 6 + i])
-        for j in range(2):
-            V0[1, 4 * i + j] = V0[1, 4 * i + j] + low
-            V0[1, 4 * i + 2 + j] = V0[1, 4 * i + 2 + j] + high
-        return carry
-
-    lax.fori_loop(0, 12, correct0, 0)
+        return [
+            (V0, (1, 4 * i + n), V0[1, 4 * i + n] + e) for n, e in ((0, low), (1, low), (2, high), (3, high))
+        ]
+
+    loop(0, 12, correct0, 2)
     sweep0(0, 4, R0 - 4)
     sweep0(1, 4, R0 - 4)
     sweep0(0, 6, R0 - 6)
@@ -720,10 +747,11 @@
     def results(r, j):
         y = r - HY
         par = odd if j % 2 == 0 else jnp.logical_not(odd)
+        stores = []
 
         def put(n, red, black):
-            tmp[n, pl.ds(y, 8, stride=2 * NY), :] = jnp.where(par, black, red)
-            tmp[n, pl.ds(NY + y, 8, stride=2 * NY), :] = jnp.where(par, red, black)
+            stores.append((tmp, (n, pl.ds(y, 8, stride=2 * NY)), jnp.where(par, black, red)))
+            stores.append((tmp, (n, pl.ds(NY + y, 8, stride=2 * NY)), jnp.where(par, red, black)))
 
         v_red, v_black = V0[0, r], V0[1, r]
         put(0, v_red[:, :128], v_black[:, :128])
@@ -731,6 +759,7 @@
         res_black = D0[1, r] * (update0(1, r, j) - v_black)
         put(1, res_red[:, :128], res_black[:, :128])
         put(2, und[0, r, :, :128], und[1, r, :, :128])
+        return stores
 
     loop(HY, HY + NY, results)
     for x in range(NX):
@@ -779,7 +808,6 @@
         vm(2, R0, 8, 256),
         vm(2, R0, 8, 128),
         vm(3, 3, 12, 8, 128),
-        vm(3, 3, 8, 8, 128),
         vm(3, 3, 4, 8, 128),
         vm(2, R1, 8, 256),
         vm(2, R1, 8, 256),
@@ -793,6 +821,9 @@
         vm(2, R2, 8, 256),
         vm(2, R2, 8, 256),
         vm(R2, 8, 256),
+        vm(R1, 8, 128),
+        vm(4, 8, 128),
+        vm(2, 12, 8, 128),
         vm(1, 1, 128),
         vm(1, 1, 128),
         vm(GY * GZ, 1, 128),
@@ -811,7 +842,7 @@
         pltpu.SemaphoreType.DMA((5,)),
         pltpu.SemaphoreType.DMA((3,)),
     ]
-    hbm = pl.BlockSpec(memory_space=pl.ANY)
+    hbm = pl.BlockSpec(memory_space=pltpu.HBM)
     return pl.pallas_call(
         functools.partial(kernel, GY, GZ),
         out_shape=(

time: 80.4 us -> 69.3 us (0.86)
  Pallas kernels: 72.8 us -> 61.7 us
    pallas_call x1, Pallas kernels: 72.8 us -> 61.7 us  [per_device(): pl.pallas_call(functools.partial(kernel, GY, GZ), out_shape=(jax.ShapeDty...]
where the time goes in v2:
time: 69.3 us; the launch traced here: 69 us
  Pallas kernels  61.7 us (89%)
  local copies, waits for them, and re-layouts  6.67 us (10%)
    pallas_call x1, Pallas kernels, per_device(): pl.pallas_call(functools.partial(kernel, GY, GZ), out_shape=(jax.ShapeDty...  61.7 us
    unnamed x13, local copies, waits for them, and re-layouts  6.67 us

profile of v2, /device:TPU:1, one launch (start us, length us, event | category | flops | bytes accessed | tf_op | source)
XLA Modules:
  0.0 69.0 jit_solution(16633520562763327700)
XLA Ops:
  0.6 0.0 copy-start
  0.6 0.9 %copy-done = f32[16,32,128]{2,1,0:T(8,128)S(1)} copy-done((f32[16,32,128]{2,1,0:T(8,128)S(1)}, f32[16,32,128]{2,1,0:T(8,128)}, u32[]{:S(2)}) %copy-start) | copy-done | bytes 262168
  1.6 0.0 copy-start.1
  1.6 0.9 %copy-done.1 = f32[16,32,128]{2,1,0:T(8,128)S(1)} copy-done((f32[16,32,128]{2,1,0:T(8,128)S(1)}, f32[16,32,128]{2,1,0:T(8,128)}, u32[]{:S(2)}) %copy-start.1) | copy-done | bytes 262168
  2.5 0.0 copy-start.2
  2.5 0.9 %copy-done.2 = bf16[16,32,128]{2,1,0:T(8,128)(2,1)S(1)} copy-done((bf16[16,32,128]{2,1,0:T(8,128)(2,1)S(1)}, bf16[16,32,128]{2,1,0:T(8,128)(2,1)}, u32[]{:S(2)}) %copy-start.2) | copy-done | bytes 131096
  3.4 0.0 copy-start.3
  3.4 0.9 %copy-done.3 = bf16[16,32,128]{2,1,0:T(8,128)(2,1)S(1)} copy-done((bf16[16,32,128]{2,1,0:T(8,128)(2,1)S(1)}, bf16[16,32,128]{2,1,0:T(8,128)(2,1)}, u32[]{:S(2)}) %copy-start.3) | copy-done | bytes 131096
  4.3 0.0 copy-start.4
  4.3 0.9 %copy-done.4 = bf16[16,32,128]{2,1,0:T(8,128)(2,1)S(1)} copy-done((bf16[16,32,128]{2,1,0:T(8,128)(2,1)S(1)}, bf16[16,32,128]{2,1,0:T(8,128)(2,1)}, u32[]{:S(2)}) %copy-start.4) | copy-done | bytes 131096
  5.2 61.7 %shard_map.76 = (bf16[16,32,128]{2,1,0:T(8,128)(2,1)S(1)}, f32[16,32,128]{2,1,0:T(8,128)S(1)}, f32[16,32,128]{2,1,0:T(8,128)S(1)}) custom-call(bf16[16,32,128]{2,1,0:T(8,128)(2,1)S(1)} %copy-done.2, bf16[16,32,128]{2,1,0:T(8,128)(2,1)S(1)} %copy-done.3, bf16[16,32,128]{2,1,0:T(8,128)(2,1)S(1)} %copy-done.4, f32[16,32,128]{2,1,0:T(8,128)S(1)} %copy-done, ...), custom_call_target="tpu_custom_call" | custom-call | tf_op jit(solution)/shard_map/pallas_call | solution.py:846
  67.0 0.7 copy.11
  67.6 0.7 %copy.12 = f32[16,32,128]{2,1,0:T(8,128)} copy(f32[16,32,128]{2,1,0:T(8,128)S(1)} %get-tuple-element.7) | data formatting | bytes 524288
  68.3 0.7 %copy.13 = f32[16,32,128]{2,1,0:T(8,128)} copy(f32[16,32,128]{2,1,0:T(8,128)S(1)} %get-tuple-element.8) | data formatting | bytes 524288
Async XLA Ops:
  0.6 1.0 %copy-start = (f32[16,32,128]{2,1,0:T(8,128)S(1)}, f32[16,32,128]{2,1,0:T(8,128)}, u32[]{:S(2)}) copy-start(f32[16,32,128]{2,1,0:T(8,128)} %src_h.1) | copy-start | bytes 786436
  1.6 0.9 %copy-start.1 = (f32[16,32,128]{2,1,0:T(8,128)S(1)}, f32[16,32,128]{2,1,0:T(8,128)}, u32[]{:S(2)}) copy-start(f32[16,32,128]{2,1,0:T(8,128)} %pres_h.1) | copy-start | bytes 786436
  2.5 0.9 %copy-start.2 = (bf16[16,32,128]{2,1,0:T(8,128)(2,1)S(1)}, bf16[16,32,128]{2,1,0:T(8,128)(2,1)}, u32[]{:S(2)}) copy-start(bf16[16,32,128]{2,1,0:T(8,128)(2,1)} %phase_h.1) | copy-start | bytes 393220
  3.4 0.9 %copy-start.3 = (bf16[16,32,128]{2,1,0:T(8,128)(2,1)S(1)}, bf16[16,32,128]{2,1,0:T(8,128)(2,1)}, u32[]{:S(2)}) copy-start(bf16[16,32,128]{2,1,0:T(8,128)(2,1)} %under_h.1) | copy-start | bytes 393220
  4.3 0.9 %copy-start.4 = (bf16[16,32,128]{2,1,0:T(8,128)(2,1)S(1)}, bf16[16,32,128]{2,1,0:T(8,128)(2,1)}, u32[]{:S(2)}) copy-start(bf16[16,32,128]{2,1,0:T(8,128)(2,1)} %perm_h.1) | copy-start | bytes 393220

commit v3 on v2

--- a/solution.py
+++ b/solution.py
@@ -44,13 +44,13 @@
 
 
 def kernel(
-    GY, GZ, phase_h, under_h, perm_h, src_h, pres_h, phase_o, pres_o, res_o,
-    inb, inf, tmp, pb, outb,
+    GY, GZ, phase_h, under_h, perm_h, src_h, pres_h, ice_o, fin_o,
+    inb, tmp, outb, outf,
     ha, hf, zp, zpf, zb, zbf,
     ice, und, prm, S0, V0, K0, G0, BD0, D0, zv,
     KX, CX, K1, V1, G1, I1, BD1, D1, K2, V2, G2, I2, BD2, D2,
     b1, zp1, zb1, msg_k, msg_b, GK, GB, K3, G3, I3, D3, buf4, e3x, pair2,
-    ssem, rsem, gs, gr, lsem, osem,
+    ssem, rsem, gs, gr, lsem, osem, known,
 ):
     gy, gz = lax.axis_index("gy"), lax.axis_index("gz")
     me = gy * GZ + gz
@@ -60,19 +60,12 @@
 
     barrier = pltpu.get_barrier_semaphore()
 
-    def other(i):
-        q = lax.rem(me + i, GY * GZ)
-        return (q // GZ, lax.rem(q, GZ))
-
-    def greet(i, carry):
-        pl.semaphore_signal(barrier, inc=1, device_id=other(i), device_id_type=MESH)
-        return carry
-
-    lax.fori_loop(1, GY * GZ, greet, 0)
+    for dy, dz in NEAR:
+        pl.semaphore_signal(barrier, inc=1, device_id=peer(dy, dz), device_id_type=MESH)
 
     loads = []
     for n, (src, dst) in enumerate(
-        ((phase_h, inb.at[0]), (under_h, inb.at[1]), (perm_h, inb.at[2]), (src_h, inf.at[0]), (pres_h, inf.at[1]))
+        ((phase_h, inb.at[0]), (under_h, inb.at[1]), (perm_h, inb.at[2]), (src_h, tmp.at[3]), (pres_h, tmp.at[4]))
     ):
         copy = pltpu.make_async_copy(src, dst, lsem.at[n])
         copy.start()
@@ -103,11 +96,7 @@
     for copy in loads:
         copy.wait()
     for n in range(3):
-        for x in range(NX):
-            tmp[n, pl.ds(x * NY, NY), :] = inb[n, x].astype(F32)
-    for n in range(2):
-        for x in range(NX):
-            tmp[3 + n, pl.ds(x * NY, NY), :] = inf[n, x]
+        tmp[n] = inb[n].astype(F32)
 
     def red_black_of(n, y, j):
         even = tmp[n, pl.ds(y, 8, stride=2 * NY), :]
@@ -141,7 +130,7 @@
 
     lax.fori_loop(0, 4, prepare, 0)
 
-    pl.semaphore_wait(barrier, GY * GZ - 1)
+    pl.semaphore_wait(barrier, len(NEAR))
 
     def exchange(ex, pieces):
         copies = []
@@ -189,6 +178,8 @@
 
     received(x_in)
     received(x_f)
+    for dy, dz in NEAR:
+        pl.semaphore_signal(known.at[0], inc=1, device_id=peer(2 * dy, 2 * dz), device_id_type=MESH)
 
     def row_mask(r, width):
         ok = ((r >= HY) | up_in) & ((r < HY + NY) | down_in)
@@ -319,13 +310,22 @@
         msg[0] = row
         landing[pl.ds(me, 1)] = row.reshape(1, 1, 128)
 
+        def start(y, z):
+            pltpu.make_async_remote_copy(
+                msg, landing.at[pl.ds(me, 1)], gs.at[n], gr.at[n], device_id=(y, z), device_id_type=MESH
+            ).start()
+
+        columns = [lax.rem(gz + i, GZ) for i in (4, 3, 5, 2, 6, 1, 7, 0)]
+
         def send(i, carry):
-            pltpu.make_async_remote_copy(
-                msg, landing.at[pl.ds(me, 1)], gs.at[n], gr.at[n], device_id=other(i), device_id_type=MESH
-            ).start()
+            y = lax.rem(gy + i, GY)
+            for z in columns:
+                start(y, z)
             return carry
 
-        lax.fori_loop(1, GY * GZ, send, 0)
+        lax.fori_loop(1, GY, send, 0)
+        for z in columns[:-1]:
+            start(gy, z)
 
     def all_bytes(landing, sem):
         part = landing.at[pl.ds(0, GY * GZ - 1)]
@@ -347,7 +347,11 @@
         black = jnp.where(low, roll(even, 4, 1), odds)
         return red.reshape(64, 128), black.reshape(64, 128)
 
-    gather(msg_k, GK, 0, message(k3_rows))
+    row_k = message(k3_rows)
+
+    pl.semaphore_wait(known.at[0], len(NEAR))
+    for dy in (-4, 4):
+        pl.semaphore_signal(known.at[1], inc=1, device_id=peer(dy, 0), device_id_type=MESH)
 
     def faces0(r, j):
         stores = []
@@ -417,6 +421,8 @@
 
     x_b1 = exchange(X_B1, b1_pieces)
 
+    pl.semaphore_wait(known.at[1], 2)
+    gather(msg_k, GK, 0, row_k)
     received(x_k)
 
     def joined(ref, yb, r):
@@ -482,65 +488,6 @@
     loop(2, R1 - 2, lambda r, j: faces_y(1, K1, G1, I1, D1, r))
     loop(1, R2 - 1, lambda r, j: faces_y(2, K2, G2, I2, D2, r))
 
-    all_bytes(GK, gr.at[0])
-    k3r, k3b = global_level3(GK)
-    row3 = lax.broadcasted_iota(jnp.int32, (64, 128), 0)
-    lane3 = lax.broadcasted_iota(jnp.int32, (64, 128), 1)
-    odd3 = (row3 + lane3) % 2 == 1
-    edges3 = (row3 == 0, row3 == 63, lane3 == 0, lane3 == 127)
-
-    def near3(o):
-        return (roll(o, 1, 0), roll(o, -1, 0), roll(o, 1, 1), roll(o, -1, 1), o)
-
-    def faces3(c, k, o):
-        s = 0.25**3
-        near = [jnp.where(e, 0.0, v) for e, v in zip(edges3, near3(o))] + [o]
-        f = [0.5 * (k + value) for value in near] + [0.5 * k]
-        d = ((f[0] + f[1]) + (f[2] + f[3])) + (f[4] + f[5])
-        inv = 1.0 / d
-        for n in range(5):
-            g = f[n] * inv
-            G3[c, n] = jnp.where(edges3[n], 0.0, g) if n < 4 else g
-        I3[c] = inv * (1.0 / s)
-        if c == 0:
-            D3[...] = s * d
-
-    faces3(0, k3r, k3b)
-    faces3(1, k3b, k3r)
-
-    lane4 = lax.broadcasted_iota(jnp.int32, (16, 128), 1)
-    row4 = lax.broadcasted_iota(jnp.int32, (16, 128), 0)
-    p4 = (lane4 // 2) % 2 == 1
-
-    def level4_of(total):
-        t = total + swap_subs(total, 1)
-        buf4[...] = 0.125 * (t + swap_lanes(t, 1))
-        low, high = buf4[pl.ds(0, 16, stride=4), :], buf4[pl.ds(2, 16, stride=4), :]
-        return split(p4, low, high)
-
-    k4 = level4_of(k3r + k3b)
-
-    def near4(c, o):
-        low, high = roll(o, 1, 0), roll(o, -1, 0)
-        outer = jnp.where(p4, high, low) if c == 0 else jnp.where(p4, low, high)
-        return (o, outer, roll(o, -2, 1), roll(o, 2, 1))
-
-    def faces4(c):
-        s = 0.25**4
-        k = k4[c]
-        take = p4 if c == 0 else jnp.logical_not(p4)
-        edges = (None, jnp.where(take, row4, 15 - row4) == 15, lane4 >= 126, lane4 < 2)
-        near = near4(c, k4[1 - c])
-        near = [v if e is None else jnp.where(e, 0.0, v) for e, v in zip(edges, near)]
-        f = [0.5 * (k + value) for value in near]
-        d = ((f[0] + f[1]) + (f[2] + f[3])) + k
-        inv = 1.0 / d
-        g = [v * inv if e is None else jnp.where(e, 0.0, v * inv) for e, v in zip(edges, f)]
-        return g, inv * (1.0 / s)
-
-    g4r, i4r = faces4(0)
-    g4b, i4b = faces4(1)
-
     received(x_b1)
 
     def v0_pieces(dy, dz):
@@ -621,6 +568,74 @@
         CX[1, 1, y] = jnp.where(lane % 4 < 2, pair2[2 + y], V2[1, 5 + y, :, :128])
     x_b2 = exchange(X_B2, block_pieces(CX))
     x_v0 = exchange(X_V0, v0_pieces)
+
+    def new_ice(r, j):
+        both = jnp.concatenate([und[0, r, :, :128], und[1, r, :, :128]], axis=0)
+        return [(outb, (r - HY,), both.astype(BF16))]
+
+    loop(HY, HY + NY, new_ice, 4)
+    copy = pltpu.make_async_copy(outb, ice_o, osem.at[4])
+    copy.start()
+    stores_out = [copy]
+    all_bytes(GK, gr.at[0])
+    k3r, k3b = global_level3(GK)
+    row3 = lax.broadcasted_iota(jnp.int32, (64, 128), 0)
+    lane3 = lax.broadcasted_iota(jnp.int32, (64, 128), 1)
+    odd3 = (row3 + lane3) % 2 == 1
+    edges3 = (row3 == 0, row3 == 63, lane3 == 0, lane3 == 127)
+
+    def near3(o):
+        return (roll(o, 1, 0), roll(o, -1, 0), roll(o, 1, 1), roll(o, -1, 1), o)
+
+    def faces3(c, k, o):
+        s = 0.25**3
+        near = [jnp.where(e, 0.0, v) for e, v in zip(edges3, near3(o))] + [o]
+        f = [0.5 * (k + value) for value in near] + [0.5 * k]
+        d = ((f[0] + f[1]) + (f[2] + f[3])) + (f[4] + f[5])
+        inv = 1.0 / d
+        for n in range(5):
+            g = f[n] * inv
+            G3[c, n] = jnp.where(edges3[n], 0.0, g) if n < 4 else g
+        I3[c] = inv * (1.0 / s)
+        if c == 0:
+            D3[...] = s * d
+
+    faces3(0, k3r, k3b)
+    faces3(1, k3b, k3r)
+
+    lane4 = lax.broadcasted_iota(jnp.int32, (16, 128), 1)
+    row4 = lax.broadcasted_iota(jnp.int32, (16, 128), 0)
+    p4 = (lane4 // 2) % 2 == 1
+
+    def level4_of(total):
+        t = total + swap_subs(total, 1)
+        buf4[...] = 0.125 * (t + swap_lanes(t, 1))
+        low, high = buf4[pl.ds(0, 16, stride=4), :], buf4[pl.ds(2, 16, stride=4), :]
+        return split(p4, low, high)
+
+    k4 = level4_of(k3r + k3b)
+
+    def near4(c, o):
+        low, high = roll(o, 1, 0), roll(o, -1, 0)
+        outer = jnp.where(p4, high, low) if c == 0 else jnp.where(p4, low, high)
+        return (o, outer, roll(o, -2, 1), roll(o, 2, 1))
+
+    def faces4(c):
+        s = 0.25**4
+        k = k4[c]
+        take = p4 if c == 0 else jnp.logical_not(p4)
+        edges = (None, jnp.where(take, row4, 15 - row4) == 15, lane4 >= 126, lane4 < 2)
+        near = near4(c, k4[1 - c])
+        near = [v if e is None else jnp.where(e, 0.0, v) for e, v in zip(edges, near)]
+        f = [0.5 * (k + value) for value in near]
+        d = ((f[0] + f[1]) + (f[2] + f[3])) + k
+        inv = 1.0 / d
+        g = [v * inv if e is None else jnp.where(e, 0.0, v * inv) for e, v in zip(edges, f)]
+        return g, inv * (1.0 / s)
+
+    g4r, i4r = faces4(0)
+    g4b, i4b = faces4(1)
+
     received(x_b2)
     for yb in range(3):
         row_ok = (up_in, True, down_in)[yb]
@@ -745,40 +760,48 @@
     sweep0(1, 6, R0 - 6)
 
     def results(r, j):
-        y = r - HY
-        par = odd if j % 2 == 0 else jnp.logical_not(odd)
         stores = []
-
-        def put(n, red, black):
-            stores.append((tmp, (n, pl.ds(y, 8, stride=2 * NY)), jnp.where(par, black, red)))
-            stores.append((tmp, (n, pl.ds(NY + y, 8, stride=2 * NY)), jnp.where(par, red, black)))
-
-        v_red, v_black = V0[0, r], V0[1, r]
-        put(0, v_red[:, :128], v_black[:, :128])
-        res_red = D0[0, r] * (update0(0, r, j) - v_red)
-        res_black = D0[1, r] * (update0(1, r, j) - v_black)
-        put(1, res_red[:, :128], res_black[:, :128])
-        put(2, und[0, r, :, :128], und[1, r, :, :128])
+        for c in range(2):
+            v = V0[c, r]
+            res = D0[c, r] * (update0(c, r, j % 2) - v)
+            stores.append((outf, (r - HY, c), v[:, :128]))
+            stores.append((outf, (r - HY, 2 + c), res[:, :128]))
         return stores
 
-    loop(HY, HY + NY, results)
-    for x in range(NX):
-        outb[x] = tmp[2, pl.ds(x * NY, NY), :].astype(BF16)
-        pb[0, x] = tmp[0, pl.ds(x * NY, NY), :]
-        pb[1, x] = tmp[1, pl.ds(x * NY, NY), :]
-    stores = []
-    for n, (src, dst) in enumerate(((outb, phase_o), (pb.at[0], pres_o), (pb.at[1], res_o))):
-        copy = pltpu.make_async_copy(src, dst, osem.at[n])
+    for k in range(4):
+        lo = 8 * k
+        loop(HY + lo, HY + lo + 8, results, 4)
+        copy = pltpu.make_async_copy(outf.at[pl.ds(lo, 8)], fin_o.at[pl.ds(lo, 8)], osem.at[k])
         copy.start()
-        stores.append(copy)
+        stores_out.append(copy)
 
     for copies in (x_in, x_f, x_k, x_b1, x_b2):
         for copy in copies:
             copy.wait_send()
     all_bytes(GK, gs.at[0])
     all_bytes(GB, gs.at[1])
-    for copy in stores:
+    for copy in stores_out:
         copy.wait()
+
+
+def unpair(ice, fin, phase_o, pres_o, res_o, tmp):
+    odd = lax.broadcasted_iota(jnp.int32, (8, 128), 1) % 2 == 1
+
+    def row(y, j):
+        par = odd if j % 2 == 0 else jnp.logical_not(odd)
+        both = ice[y].astype(F32)
+        stores = []
+        for ref, red, black in (
+            (tmp, both[:8], both[8:]),
+            (pres_o, fin[y, 0], fin[y, 1]),
+            (res_o, fin[y, 2], fin[y, 3]),
+        ):
+            stores.append((ref, (pl.ds(y, 8, stride=2 * NY), slice(None)), jnp.where(par, black, red)))
+            stores.append((ref, (pl.ds(NY + y, 8, stride=2 * NY), slice(None)), jnp.where(par, red, black)))
+        return stores
+
+    loop(0, NY, row, 4)
+    phase_o[...] = tmp[...].astype(BF16)
 
 
 def per_device(GY, GZ, phase, undercool, perm_base, source, pressure):
@@ -786,11 +809,10 @@
         return pltpu.VMEM(shape, F32)
 
     scratch = [
-        pltpu.VMEM((3, NX, NY, NZ), BF16),
-        vm(2, NX, NY, NZ),
+        pltpu.VMEM((3, NX * NY, NZ), BF16),
         vm(5, NX * NY, NZ),
-        vm(2, NX, NY, NZ),
-        pltpu.VMEM((NX, NY, NZ), BF16),
+        pltpu.VMEM((NY, 16, 128), BF16),
+        vm(NY, 4, 8, 128),
         pltpu.VMEM((R0, 48, 128), BF16),
         vm(R0, 24, 128),
         pltpu.VMEM((4, 48, 128), BF16),
@@ -840,23 +862,35 @@
         pltpu.SemaphoreType.DMA((2,)),
         pltpu.SemaphoreType.DMA((2,)),
         pltpu.SemaphoreType.DMA((5,)),
-        pltpu.SemaphoreType.DMA((3,)),
+        pltpu.SemaphoreType.DMA((5,)),
+        pltpu.SemaphoreType.REGULAR((2,)),
     ]
     hbm = pl.BlockSpec(memory_space=pltpu.HBM)
-    return pl.pallas_call(
+    vmem = pl.BlockSpec(memory_space=pltpu.VMEM)
+    flat = (NX * NY, NZ)
+    packed_ice, packed = pl.pallas_call(
         functools.partial(kernel, GY, GZ),
-        out_shape=(
-            jax.ShapeDtypeStruct((NX, NY, NZ), BF16),
-            jax.ShapeDtypeStruct((NX, NY, NZ), F32),
-            jax.ShapeDtypeStruct((NX, NY, NZ), F32),
-        ),
+        out_shape=(jax.ShapeDtypeStruct((NY, 16, NZ), BF16), jax.ShapeDtypeStruct((NY, 4, 8, NZ), F32)),
         in_specs=[hbm] * 5,
-        out_specs=(hbm, hbm, hbm),
+        out_specs=(hbm, hbm),
         scratch_shapes=scratch,
         compiler_params=pltpu.CompilerParams(
-            collective_id=0, has_side_effects=True, vmem_limit_bytes=48 * 2**20
+            collective_id=0, has_side_effects=True, vmem_limit_bytes=63 * 2**20
         ),
-    )(phase, undercool, perm_base, source, pressure)
+    )(*[a.reshape(flat) for a in (phase, undercool, perm_base, source, pressure)])
+    outs = pl.pallas_call(
+        unpair,
+        out_shape=(
+            jax.ShapeDtypeStruct(flat, BF16),
+            jax.ShapeDtypeStruct(flat, F32),
+            jax.ShapeDtypeStruct(flat, F32),
+        ),
+        in_specs=[vmem] * 2,
+        out_specs=(vmem, vmem, vmem),
+        scratch_shapes=[vm(NX * NY, NZ)],
+        compiler_params=pltpu.CompilerParams(vmem_limit_bytes=63 * 2**20),
+    )(packed_ice, packed)
+    return tuple(a.reshape(NX, NY, NZ) for a in outs)
 
 
 def solution(mesh):

time: 69.3 us -> 58.4 us (0.84)
  local copies, waits for them, and re-layouts: 6.67 us -> 0 us
  Pallas kernels: 61.7 us -> 57.3 us
    pallas_call x1, Pallas kernels: 61.7 us -> 54.6 us  [per_device(): pl.pallas_call(functools.partial(kernel, GY, GZ), out_shape=(jax.ShapeDty...]
    unnamed x13 -> x0, local copies, waits for them, and re-layouts: 6.67 us -> none
    pallas_call x0 -> x1, Pallas kernels: none -> 2.71 us  [per_device(): pl.pallas_call(unpair, out_shape=(jax.ShapeDtypeStruct(flat, BF16), jax.S...]
where the time goes in v3:
time: 58.4 us; the launch traced here: 58 us
  Pallas kernels  57.3 us (98%)
  between operations  0.64 us (1%)
    pallas_call x1, Pallas kernels, per_device(): pl.pallas_call(functools.partial(kernel, GY, GZ), out_shape=(jax.ShapeDty...  54.6 us
    pallas_call x1, Pallas kernels, per_device(): pl.pallas_call(unpair, out_shape=(jax.ShapeDtypeStruct(flat, BF16), jax.S...  2.71 us

profile of v3, /device:TPU:1, one launch (start us, length us, event | category | flops | bytes accessed | tf_op | source)
XLA Modules:
  0.0 58.0 jit_solution(3977221525749545922)
XLA Ops:
  0.6 54.6 %shard_map.76 = (bf16[32,16,128]{2,1,0:T(8,128)(2,1)}, f32[32,4,8,128]{3,2,1,0:T(8,128)}) custom-call(bf16[512,128]{1,0:T(8,128)(2,1)} %bitcast.10, bf16[512,128]{1,0:T(8,128)(2,1)} %bitcast.11, bf16[512,128]{1,0:T(8,128)(2,1)} %bitcast.12, f32[512,128]{1,0:T(8,128)} %bitcast.8, f32[512,128]{1,0:T(8,128)} %bitcast.9), custom_call_target="tpu_custom_call" | custom-call | tf_op jit(solution)/shard_map/pallas_call | solution.py:871
  55.2 2.7 %shard_map.77 = (bf16[512,128]{1,0:T(8,128)(2,1)}, f32[512,128]{1,0:T(8,128)}, f32[512,128]{1,0:T(8,128)}) custom-call(bf16[32,16,128]{2,1,0:T(8,128)(2,1)} %get-tuple-element.8.ice, f32[32,4,8,128]{3,2,1,0:T(8,128)} %get-tuple-element.9.fin), custom_call_target="tpu_custom_call" | custom-call | tf_op jit(solution)/shard_map/pallas_call | solution.py:881

commit v4 on v3

--- a/solution.py
+++ b/solution.py
@@ -228,6 +228,7 @@
         return (ref[1 - c, r - 1], ref[1 - c, r + 1], o, x_outer(o, take), ahead, behind)
 
     def permeability(r, j):
+        j = j % 2
         stores = []
         for c in range(2):
             now = ice[c, r]
@@ -244,7 +245,7 @@
             stores.append((und, (c, r), new))
         return stores
 
-    loop(2, R0 - 2, permeability)
+    loop(2, R0 - 2, permeability, 4)
 
     def swap_lanes(x, d):
         return jnp.where((lax.broadcasted_iota(jnp.int32, x.shape, 1) // d) % 2 == 0, roll(x, -d, 1), roll(x, d, 1))
@@ -354,6 +355,7 @@
         pl.semaphore_signal(known.at[1], inc=1, device_id=peer(dy, 0), device_id_type=MESH)
 
     def faces0(r, j):
+        j = j % 2
         stores = []
         ok = row_mask(r, 5)
         for c in range(2):
@@ -372,7 +374,7 @@
             stores.append((D0, (c, r), d))
         return stores
 
-    loop(4, R0 - 4, faces0)
+    loop(4, R0 - 4, faces0, 4)
 
     def update0(c, r, j):
         near = near0(V0, c, r, j)
@@ -383,7 +385,7 @@
         def body(r, j):
             return [(V0, (c, r), update0(c, r, j % 2))]
 
-        loop(lo, hi, body, 4)
+        loop(lo, hi, body, 10 if hi - lo == 40 else 12)
 
     sweep0(0, 4, R0 - 4)
     sweep0(1, 4, R0 - 4)
@@ -510,7 +512,7 @@
             stores.append((V1, (0, r), stores[-2][2]))
         return stores
 
-    loop(1, 11, spread_b, 2)
+    loop(1, 11, spread_b, 10)
 
     def update_y(level, V, G, BD, c, r):
         near = near_y(level, V, c, r)
@@ -521,7 +523,7 @@
         def body(r, j):
             return [(V, (c, r), update_y(level, V, G, BD, c, r))]
 
-        loop(lo, hi, body, 4)
+        loop(lo, hi, body, hi - lo)
 
     sweep_y(1, V1, G1, BD1, 1, 2, 22)
     sweep_y(1, V1, G1, BD1, 0, 2, 22)
@@ -551,7 +553,7 @@
     V2[0, 11] = zero_row
     V2[1, 2] = zero_row
     V2[1, 11] = zero_row
-    loop(0, 8, right2, 2)
+    loop(0, 8, right2, 8)
 
     sweep_y(2, V2, G2, BD2, 1, 3, 11)
     sweep_y(2, V2, G2, BD2, 0, 3, 11)

time: 58.4 us -> 49.8 us (0.85)
  Pallas kernels: 57.3 us -> 49 us
    pallas_call x1, Pallas kernels: 54.6 us -> 46.3 us  [per_device(): pl.pallas_call(functools.partial(kernel, GY, GZ), out_shape=(jax.ShapeDty...]
where the time goes in v4:
time: 49.8 us; the launch traced here: 49.6 us
  Pallas kernels  49 us (98%)
  between operations  0.64 us (1%)
    pallas_call x1, Pallas kernels, per_device(): pl.pallas_call(functools.partial(kernel, GY, GZ), out_shape=(jax.ShapeDty...  46.3 us
    pallas_call x1, Pallas kernels, per_device(): pl.pallas_call(unpair, out_shape=(jax.ShapeDtypeStruct(flat, BF16), jax.S...  2.71 us

profile of v4, /device:TPU:1, one launch (start us, length us, event | category | flops | bytes accessed | tf_op | source)
XLA Modules:
  0.0 49.6 jit_solution(14703549603353500143)
XLA Ops:
  0.6 46.3 %shard_map.76 = (bf16[32,16,128]{2,1,0:T(8,128)(2,1)}, f32[32,4,8,128]{3,2,1,0:T(8,128)}) custom-call(bf16[512,128]{1,0:T(8,128)(2,1)} %bitcast.10, bf16[512,128]{1,0:T(8,128)(2,1)} %bitcast.11, bf16[512,128]{1,0:T(8,128)(2,1)} %bitcast.12, f32[512,128]{1,0:T(8,128)} %bitcast.8, f32[512,128]{1,0:T(8,128)} %bitcast.9), custom_call_target="tpu_custom_call" | custom-call | tf_op jit(solution)/shard_map/pallas_call | solution.py:873
  46.9 2.7 %shard_map.77 = (bf16[512,128]{1,0:T(8,128)(2,1)}, f32[512,128]{1,0:T(8,128)}, f32[512,128]{1,0:T(8,128)}) custom-call(bf16[32,16,128]{2,1,0:T(8,128)(2,1)} %get-tuple-element.8.ice, f32[32,4,8,128]{3,2,1,0:T(8,128)} %get-tuple-element.9.fin), custom_call_target="tpu_custom_call" | custom-call | tf_op jit(solution)/shard_map/pallas_call | solution.py:883

commit v5 on v4

--- a/solution.py
+++ b/solution.py
@@ -177,7 +177,6 @@
             V0[c, r] = zero_row
 
     received(x_in)
-    received(x_f)
     for dy, dz in NEAR:
         pl.semaphore_signal(known.at[0], inc=1, device_id=peer(2 * dy, 2 * dz), device_id_type=MESH)
 
@@ -189,15 +188,12 @@
     def unpack(k, carry):
         group = lax.broadcasted_iota(jnp.int32, (48, 128), 1) % 16 < 8
         merged = jnp.where(group, zb[0, k].astype(F32), zb[1, k].astype(F32))
-        merged_f = jnp.where(group[:24], zbf[0, k], zbf[1, k])
         for q in range(8):
             r = 8 * k + q
             ok = row_mask(r, 6) & (r >= 2) & (r < R0 - 2)
             ok5 = row_mask(r, 5) & (r >= 3) & (r < R0 - 3)
             side = roll(merged, 120 - 16 * q, 1)
-            side_f = roll(merged_f, 120 - 16 * q, 1)
             a = ha[r].astype(F32)
-            f = hf[r]
             for c in range(2):
                 s = slice(8 * c, 8 * c + 8)
                 ice[c, r] = jnp.where(ok, cat(a[s], side[s]), 0.0)
@@ -205,9 +201,20 @@
                 und[c, r] = cat(a[s], side[s])
                 s = slice(32 + 8 * c, 40 + 8 * c)
                 prm[c, r] = jnp.where(ok5, cat(a[s], side[s]), 0.0)
+        return carry
+
+    def unpack_f(k, carry):
+        group = lax.broadcasted_iota(jnp.int32, (24, 128), 1) % 16 < 8
+        merged = jnp.where(group, zbf[0, k], zbf[1, k])
+        for q in range(8):
+            r = 8 * k + q
+            ok5 = row_mask(r, 5) & (r >= 3) & (r < R0 - 3)
+            side = roll(merged, 120 - 16 * q, 1)
+            f = hf[r]
+            for c in range(2):
                 s = slice(8 * c, 8 * c + 8)
-                S0[c, r] = cat(f[s], side_f[s])
-            V0[1, r] = jnp.where(ok5, cat(f[16:24], side_f[16:24]), 0.0)
+                S0[c, r] = cat(f[s], side[s])
+            V0[1, r] = jnp.where(ok5, cat(f[16:24], side[16:24]), 0.0)
         return carry
 
     lax.fori_loop(0, 6, unpack, 0)
@@ -349,6 +356,9 @@
         return red.reshape(64, 128), black.reshape(64, 128)
 
     row_k = message(k3_rows)
+
+    received(x_f)
+    lax.fori_loop(0, 6, unpack_f, 0)
 
     pl.semaphore_wait(known.at[0], len(NEAR))
     for dy in (-4, 4):
@@ -638,6 +648,22 @@
     g4r, i4r = faces4(0)
     g4b, i4b = faces4(1)
 
+    def shifts4(o):
+        return near4(1, o)
+
+    back4 = [shifts4(g) for g in g4r]
+    m4 = (
+        (g4b[0] * back4[0][0] + g4b[1] * back4[1][1]) + (g4b[2] * back4[3][2] + g4b[3] * back4[2][3]),
+        g4b[0] * back4[1][0],
+        g4b[1] * back4[0][1],
+        g4b[0] * back4[2][0] + g4b[2] * back4[0][2],
+        g4b[0] * back4[3][0] + g4b[3] * back4[0][3],
+        g4b[1] * back4[2][1] + g4b[2] * back4[1][2],
+        g4b[1] * back4[3][1] + g4b[3] * back4[1][3],
+        g4b[2] * back4[2][2],
+        g4b[3] * back4[3][3],
+    )
+
     received(x_b2)
     for yb in range(3):
         row_ok = (up_in, True, down_in)[yb]
@@ -701,14 +727,27 @@
         near = near4(c, o)
         return bd + ((g[0] * near[0] + g[1] * near[1]) + (g[2] * near[2] + g[3] * near[3]))
 
-    def sweep4(i, carry):
-        red, black = carry
-        red = update4(0, g4r, bd4r, black)
-        black = update4(1, g4b, bd4b, red)
-        return red, black
-
-    zero4 = jnp.zeros((16, 128), F32)
-    e_r, e_b = lax.fori_loop(0, COARSE_SWEEPS, sweep4, (zero4, zero4))
+    c4 = update4(1, g4b, bd4b, bd4r)
+
+    def sweep4(i, black):
+        low, high = roll(black, 1, 0), roll(black, -1, 0)
+        outer, inner = jnp.where(p4, high, low), jnp.where(p4, low, high)
+        t = [
+            m * v
+            for m, v in zip(
+                m4,
+                (
+                    black, outer, inner, roll(black, -2, 1), roll(black, 2, 1),
+                    roll(outer, -2, 1), roll(outer, 2, 1), roll(black, -4, 1), roll(black, 4, 1),
+                ),
+            )
+        ]
+        near = ((c4 + t[0]) + (t[1] + t[2])) + ((t[3] + t[4]) + (t[7] + t[8]))
+        return near + (t[5] + t[6])
+
+    black4 = lax.fori_loop(0, COARSE_SWEEPS - 2, sweep4, c4)
+    e_r = update4(0, g4r, bd4r, black4)
+    e_b = update4(1, g4b, bd4b, e_r)
     low, high = split(p4, e_r, e_b)
     buf4[pl.ds(0, 16, stride=4), :] = low
     buf4[pl.ds(1, 16, stride=4), :] = low
@@ -766,14 +805,14 @@
         for c in range(2):
             v = V0[c, r]
             res = D0[c, r] * (update0(c, r, j % 2) - v)
-            stores.append((outf, (r - HY, c), v[:, :128]))
-            stores.append((outf, (r - HY, 2 + c), res[:, :128]))
+            stores.append((outf, (0, r - HY, c), v[:, :128]))
+            stores.append((outf, (1, r - HY, c), res[:, :128]))
         return stores
 
     for k in range(4):
         lo = 8 * k
-        loop(HY + lo, HY + lo + 8, results, 4)
-        copy = pltpu.make_async_copy(outf.at[pl.ds(lo, 8)], fin_o.at[pl.ds(lo, 8)], osem.at[k])
+        loop(HY + lo, HY + lo + 8, results, 8)
+        copy = pltpu.make_async_copy(outf.at[:, pl.ds(lo, 8)], fin_o.at[:, pl.ds(lo, 8)], osem.at[k])
         copy.start()
         stores_out.append(copy)
 
@@ -786,24 +825,38 @@
         copy.wait()
 
 
-def unpair(ice, fin, phase_o, pres_o, res_o, tmp):
+def unpair(ice_h, fin_h, phase_o, pres_o, res_o, ice, fin, tmp, narrow, isem, osem):
+    loads = [
+        pltpu.make_async_copy(src, dst, isem.at[n])
+        for n, (src, dst) in enumerate(((ice_h, ice), (fin_h.at[0], fin.at[0]), (fin_h.at[1], fin.at[1])))
+    ]
+    for copy in loads:
+        copy.start()
     odd = lax.broadcasted_iota(jnp.int32, (8, 128), 1) % 2 == 1
-
-    def row(y, j):
-        par = odd if j % 2 == 0 else jnp.logical_not(odd)
-        both = ice[y].astype(F32)
-        stores = []
-        for ref, red, black in (
-            (tmp, both[:8], both[8:]),
-            (pres_o, fin[y, 0], fin[y, 1]),
-            (res_o, fin[y, 2], fin[y, 3]),
-        ):
-            stores.append((ref, (pl.ds(y, 8, stride=2 * NY), slice(None)), jnp.where(par, black, red)))
-            stores.append((ref, (pl.ds(NY + y, 8, stride=2 * NY), slice(None)), jnp.where(par, red, black)))
-        return stores
-
-    loop(0, NY, row, 4)
-    phase_o[...] = tmp[...].astype(BF16)
+    stores = []
+    for n, out in enumerate((phase_o, pres_o, res_o)):
+        loads[n].wait()
+
+        def row(y, j, n=n):
+            par = odd if j % 2 == 0 else jnp.logical_not(odd)
+            if n == 0:
+                both = ice[y].astype(F32)
+                red, black = both[:8], both[8:]
+            else:
+                red, black = fin[n - 1, y, 0], fin[n - 1, y, 1]
+            return [
+                (tmp, (n, pl.ds(y, 8, stride=2 * NY), slice(None)), jnp.where(par, black, red)),
+                (tmp, (n, pl.ds(NY + y, 8, stride=2 * NY), slice(None)), jnp.where(par, red, black)),
+            ]
+
+        loop(0, NY, row, 16)
+        if n == 0:
+            narrow[...] = tmp[0].astype(BF16)
+        copy = pltpu.make_async_copy(narrow if n == 0 else tmp.at[n], out, osem.at[n])
+        copy.start()
+        stores.append(copy)
+    for copy in stores:
+        copy.wait()
 
 
 def per_device(GY, GZ, phase, undercool, perm_base, source, pressure):
@@ -814,7 +867,7 @@
         pltpu.VMEM((3, NX * NY, NZ), BF16),
         vm(5, NX * NY, NZ),
         pltpu.VMEM((NY, 16, 128), BF16),
-        vm(NY, 4, 8, 128),
+        vm(2, NY, 2, 8, 128),
         pltpu.VMEM((R0, 48, 128), BF16),
         vm(R0, 24, 128),
         pltpu.VMEM((4, 48, 128), BF16),
@@ -868,11 +921,10 @@
         pltpu.SemaphoreType.REGULAR((2,)),
     ]
     hbm = pl.BlockSpec(memory_space=pltpu.HBM)
-    vmem = pl.BlockSpec(memory_space=pltpu.VMEM)
     flat = (NX * NY, NZ)
     packed_ice, packed = pl.pallas_call(
         functools.partial(kernel, GY, GZ),
-        out_shape=(jax.ShapeDtypeStruct((NY, 16, NZ), BF16), jax.ShapeDtypeStruct((NY, 4, 8, NZ), F32)),
+        out_shape=(jax.ShapeDtypeStruct((NY, 16, NZ), BF16), jax.ShapeDtypeStruct((2, NY, 2, 8, NZ), F32)),
         in_specs=[hbm] * 5,
         out_specs=(hbm, hbm),
         scratch_shapes=scratch,
@@ -887,9 +939,16 @@
             jax.ShapeDtypeStruct(flat, F32),
             jax.ShapeDtypeStruct(flat, F32),
         ),
-        in_specs=[vmem] * 2,
-        out_specs=(vmem, vmem, vmem),
-        scratch_shapes=[vm(NX * NY, NZ)],
+        in_specs=[hbm] * 2,
+        out_specs=(hbm, hbm, hbm),
+        scratch_shapes=[
+            pltpu.VMEM((NY, 16, NZ), BF16),
+            vm(2, NY, 2, 8, NZ),
+            vm(3, NX * NY, NZ),
+            pltpu.VMEM(flat, BF16),
+            pltpu.SemaphoreType.DMA((3,)),
+            pltpu.SemaphoreType.DMA((3,)),
+        ],
         compiler_params=pltpu.CompilerParams(vmem_limit_bytes=63 * 2**20),
     )(packed_ice, packed)
     return tuple(a.reshape(NX, NY, NZ) for a in outs)

time: 49.8 us -> 46.8 us (0.940)
  Pallas kernels: 49 us -> 46 us
    pallas_call x1, Pallas kernels: 46.3 us -> 43.6 us  [per_device(): pl.pallas_call(functools.partial(kernel, GY, GZ), out_shape=(jax.ShapeDty...]
where the time goes in v5:
time: 46.8 us; the launch traced here: 46.6 us
  Pallas kernels  46 us (98%)
  between operations  0.64 us (1%)
    pallas_call x1, Pallas kernels, per_device(): pl.pallas_call(functools.partial(kernel, GY, GZ), out_shape=(jax.ShapeDty...  43.6 us
    pallas_call x1, Pallas kernels, per_device(): pl.pallas_call(unpair, out_shape=(jax.ShapeDtypeStruct(flat, BF16), jax.S...  2.33 us

profile of v5, /device:TPU:1, one launch (start us, length us, event | category | flops | bytes accessed | tf_op | source)
XLA Modules:
  0.0 46.6 jit_solution(7073199938379620689)
XLA Ops:
  0.6 43.6 %shard_map.76 = (bf16[32,16,128]{2,1,0:T(8,128)(2,1)}, f32[2,32,2,8,128]{4,3,2,1,0:T(8,128)}) custom-call(bf16[512,128]{1,0:T(8,128)(2,1)} %bitcast.10, bf16[512,128]{1,0:T(8,128)(2,1)} %bitcast.11, bf16[512,128]{1,0:T(8,128)(2,1)} %bitcast.12, f32[512,128]{1,0:T(8,128)} %bitcast.8, f32[512,128]{1,0:T(8,128)} %bitcast.9), custom_call_target="tpu_custom_call" | custom-call | tf_op jit(solution)/shard_map/pallas_call | solution.py:925
  44.3 2.3 %shard_map.77 = (bf16[512,128]{1,0:T(8,128)(2,1)}, f32[512,128]{1,0:T(8,128)}, f32[512,128]{1,0:T(8,128)}) custom-call(bf16[32,16,128]{2,1,0:T(8,128)(2,1)} %get-tuple-element.8.ice_h, f32[2,32,2,8,128]{4,3,2,1,0:T(8,128)} %get-tuple-element.9.fin_h), custom_call_target="tpu_custom_call" | custom-call | tf_op jit(solution)/shard_map/pallas_call | solution.py:935

commit v6 on v5

--- a/solution.py
+++ b/solution.py
@@ -93,9 +93,8 @@
         behind = cat(jnp.where(start, bb, ba), jnp.where(start, ba, bb))
         return ahead, behind
 
-    for copy in loads:
-        copy.wait()
     for n in range(3):
+        loads[n].wait()
         tmp[n] = inb[n].astype(F32)
 
     def red_black_of(n, y, j):
@@ -104,33 +103,34 @@
         par = odd if j % 2 == 0 else jnp.logical_not(odd)
         return jnp.where(par, odds, even), jnp.where(par, even, odds)
 
-    zp[...] = jnp.zeros_like(zp)
-    zpf[...] = jnp.zeros_like(zpf)
-
-    def prepare(k, carry):
-        packed = jnp.zeros((48, 128), F32)
-        packed_f = jnp.zeros((24, 128), F32)
-        group = lax.broadcasted_iota(jnp.int32, (48, 128), 1) // 16
-        for q in range(8):
-            y = 8 * k + q
-            parts = []
-            for n in range(3):
-                parts.extend(red_black_of(n, y, q))
-            row = jnp.concatenate(parts, axis=0)
-            ha[HY + y] = row.astype(BF16)
-            s_r, s_b = red_black_of(3, y, q)
-            _, v_b = red_black_of(4, y, q)
-            row_f = jnp.concatenate([s_r, s_b, v_b], axis=0)
-            hf[HY + y] = row_f
-            packed = jnp.where(group == q, roll(row, 16 * q + 8, 1), packed)
-            packed_f = jnp.where(group[:24] == q, roll(row_f, 16 * q + 8, 1), packed_f)
-        zp[k] = packed.astype(BF16)
-        zpf[k] = packed_f
-        return carry
-
-    lax.fori_loop(0, 4, prepare, 0)
-
+    def prepare(rows, packed_rows, high, parts_of):
+        group = lax.broadcasted_iota(jnp.int32, (high, 128), 1) // 16
+
+        def block(k, carry):
+            packed = jnp.zeros((high, 128), F32)
+            stores = []
+            for q in range(8):
+                y = 8 * k + q
+                row = jnp.concatenate(parts_of(y, q), axis=0)
+                stores.append((HY + y, row))
+                packed = jnp.where(group == q, roll(row, 16 * q + 8, 1), packed)
+            for r, row in stores:
+                rows[r] = row.astype(rows.dtype)
+            packed_rows[k] = packed.astype(rows.dtype)
+            return carry
+
+        lax.fori_loop(0, 4, block, 0)
+
+    def parts_in(y, q):
+        return red_black_of(0, y, q) + red_black_of(1, y, q) + red_black_of(2, y, q)
+
+    def parts_f(y, q):
+        return red_black_of(3, y, q) + red_black_of(4, y, q)[1:]
+
+    prepare(ha, zp, 48, parts_in)
     pl.semaphore_wait(barrier, len(NEAR))
+    for dy, dz in NEAR:
+        pl.semaphore_signal(known.at[2], inc=1, device_id=peer(dy, dz), device_id_type=MESH)
 
     def exchange(ex, pieces):
         copies = []
@@ -163,6 +163,9 @@
         return pieces
 
     x_in = exchange(X_IN, input_pieces(ha, zp, zb, 6))
+    loads[3].wait()
+    loads[4].wait()
+    prepare(hf, zpf, 24, parts_f)
     x_f = exchange(X_F, input_pieces(hf, zpf, zbf, 5))
 
     zero_row = jnp.zeros((8, 256), F32)
@@ -176,10 +179,11 @@
         for r in (3, R0 - 4):
             V0[c, r] = zero_row
 
-    received(x_in)
+    pl.semaphore_wait(known.at[2], len(NEAR))
     for dy, dz in NEAR:
         pl.semaphore_signal(known.at[0], inc=1, device_id=peer(2 * dy, 2 * dz), device_id_type=MESH)
 
+    received(x_in)
     def row_mask(r, width):
         ok = ((r >= HY) | up_in) & ((r < HY + NY) | down_in)
         lanes = (lane2 < 128) | ((lane2 < 128 + width) & right_in) | ((lane2 >= 256 - width) & left_in)
@@ -217,7 +221,8 @@
             V0[1, r] = jnp.where(ok5, cat(f[16:24], side[16:24]), 0.0)
         return carry
 
-    lax.fori_loop(0, 6, unpack, 0)
+    for k in range(6):
+        unpack(k, 0)
 
     def pick(c, j):
         return odd2 if (c + j) % 2 == 0 else jnp.logical_not(odd2)
@@ -252,7 +257,7 @@
             stores.append((und, (c, r), new))
         return stores
 
-    loop(2, R0 - 2, permeability, 4)
+    loop(2, R0 - 2, permeability, 22)
 
     def swap_lanes(x, d):
         return jnp.where((lax.broadcasted_iota(jnp.int32, x.shape, 1) // d) % 2 == 0, roll(x, -d, 1), roll(x, d, 1))
@@ -433,8 +438,6 @@
 
     x_b1 = exchange(X_B1, b1_pieces)
 
-    pl.semaphore_wait(known.at[1], 2)
-    gather(msg_k, GK, 0, row_k)
     received(x_k)
 
     def joined(ref, yb, r):
@@ -499,6 +502,9 @@
 
     loop(2, R1 - 2, lambda r, j: faces_y(1, K1, G1, I1, D1, r))
     loop(1, R2 - 1, lambda r, j: faces_y(2, K2, G2, I2, D2, r))
+
+    pl.semaphore_wait(known.at[1], 2)
+    gather(msg_k, GK, 0, row_k)
 
     received(x_b1)
 
@@ -918,7 +924,7 @@
         pltpu.SemaphoreType.DMA((2,)),
         pltpu.SemaphoreType.DMA((5,)),
         pltpu.SemaphoreType.DMA((5,)),
-        pltpu.SemaphoreType.REGULAR((2,)),
+        pltpu.SemaphoreType.REGULAR((3,)),
     ]
     hbm = pl.BlockSpec(memory_space=pltpu.HBM)
     flat = (NX * NY, NZ)

time: 46.8 us -> 45.8 us (0.979)
  Pallas kernels: 46 us -> 45 us
    pallas_call x1, Pallas kernels: 43.6 us -> 42.6 us  [per_device(): pl.pallas_call(functools.partial(kernel, GY, GZ), out_shape=(jax.ShapeDty...]
where the time goes in v6:
time: 45.8 us; the launch traced here: 45.6 us
  Pallas kernels  45 us (98%)
  between operations  0.64 us (1%)
    pallas_call x1, Pallas kernels, per_device(): pl.pallas_call(functools.partial(kernel, GY, GZ), out_shape=(jax.ShapeDty...  42.6 us
    pallas_call x1, Pallas kernels, per_device(): pl.pallas_call(unpair, out_shape=(jax.ShapeDtypeStruct(flat, BF16), jax.S...  2.33 us

profile of v6, /device:TPU:1, one launch (start us, length us, event | category | flops | bytes accessed | tf_op | source)
XLA Modules:
  0.0 45.6 jit_solution(18224287919818598113)
XLA Ops:
  0.6 42.6 %shard_map.76 = (bf16[32,16,128]{2,1,0:T(8,128)(2,1)}, f32[2,32,2,8,128]{4,3,2,1,0:T(8,128)}) custom-call(bf16[512,128]{1,0:T(8,128)(2,1)} %bitcast.10, bf16[512,128]{1,0:T(8,128)(2,1)} %bitcast.11, bf16[512,128]{1,0:T(8,128)(2,1)} %bitcast.12, f32[512,128]{1,0:T(8,128)} %bitcast.8, f32[512,128]{1,0:T(8,128)} %bitcast.9), custom_call_target="tpu_custom_call" | custom-call | tf_op jit(solution)/shard_map/pallas_call | solution.py:931
  43.3 2.3 %shard_map.77 = (bf16[512,128]{1,0:T(8,128)(2,1)}, f32[512,128]{1,0:T(8,128)}, f32[512,128]{1,0:T(8,128)}) custom-call(bf16[32,16,128]{2,1,0:T(8,128)(2,1)} %get-tuple-element.8.ice_h, f32[2,32,2,8,128]{4,3,2,1,0:T(8,128)} %get-tuple-element.9.fin_h), custom_call_target="tpu_custom_call" | custom-call | tf_op jit(solution)/shard_map/pallas_call | solution.py:941

commit v7 on v6

--- a/solution.py
+++ b/solution.py
@@ -119,7 +119,8 @@
             packed_rows[k] = packed.astype(rows.dtype)
             return carry
 
-        lax.fori_loop(0, 4, block, 0)
+        for k in range(4):
+            block(k, 0)
 
     def parts_in(y, q):
         return red_black_of(0, y, q) + red_black_of(1, y, q) + red_black_of(2, y, q)

time: 45.8 us -> 45.6 us (level)
  no operation moved by 1% of the time
where the time goes in v7:
time: 45.6 us; the launch traced here: 45.4 us
  Pallas kernels  44.8 us (98%)
  between operations  0.64 us (1%)
    pallas_call x1, Pallas kernels, per_device(): pl.pallas_call(functools.partial(kernel, GY, GZ), out_shape=(jax.ShapeDty...  42.4 us
    pallas_call x1, Pallas kernels, per_device(): pl.pallas_call(unpair, out_shape=(jax.ShapeDtypeStruct(flat, BF16), jax.S...  2.33 us

profile of v7, /device:TPU:1, one launch (start us, length us, event | category | flops | bytes accessed | tf_op | source)
XLA Modules:
  0.0 45.4 jit_solution(9545251439424363981)
XLA Ops:
  0.6 42.4 %shard_map.76 = (bf16[32,16,128]{2,1,0:T(8,128)(2,1)}, f32[2,32,2,8,128]{4,3,2,1,0:T(8,128)}) custom-call(bf16[512,128]{1,0:T(8,128)(2,1)} %bitcast.10, bf16[512,128]{1,0:T(8,128)(2,1)} %bitcast.11, bf16[512,128]{1,0:T(8,128)(2,1)} %bitcast.12, f32[512,128]{1,0:T(8,128)} %bitcast.8, f32[512,128]{1,0:T(8,128)} %bitcast.9), custom_call_target="tpu_custom_call" | custom-call | tf_op jit(solution)/shard_map/pallas_call | solution.py:932
  43.1 2.3 %shard_map.77 = (bf16[512,128]{1,0:T(8,128)(2,1)}, f32[512,128]{1,0:T(8,128)}, f32[512,128]{1,0:T(8,128)}) custom-call(bf16[32,16,128]{2,1,0:T(8,128)(2,1)} %get-tuple-element.8.ice_h, f32[2,32,2,8,128]{4,3,2,1,0:T(8,128)} %get-tuple-element.9.fin_h), custom_call_target="tpu_custom_call" | custom-call | tf_op jit(solution)/shard_map/pallas_call | solution.py:942
